TPU v7x, 128 devices: a whole 4x4x4 slice. The times are simulated.
128 devices in a mesh: section: 2 (over y_lo), dp: 64 (over z, y_hi, x, core).
Axes of the slice: x: 4, y: 4 (y_hi: 2, y_lo: 2; y = y_hi * 2 + y_lo), z: 4, core: 2. Of those that a mesh axis runs over, the one named last changes fastest.
Arguments:
- tokens: bfloat16 [2, 8192, 1536], P(None, 'dp'), may hold values from -6 to 6
- cotangent: bfloat16 [2, 8192, 1536], P(None, 'dp'), may hold values from -6 to 6
- starts: int32 [2, 64, 4], P(None, 'dp'), may hold values from 0 to 128, as said below
- norm_gain: bfloat16 [2, 1536], P('section', 'dp'), may hold values from 0.5 to 1.5
- w_in: bfloat16 [2, 1536, 6448], P('section', 'dp'), may hold values from -0.15625 to 0.15625
- conv_weight: bfloat16 [2, 4, 3328], P('section', None, 'dp'), may hold values from -3 to 3
- conv_bias: bfloat16 [2, 3328], P('section', 'dp'), may hold values from -1.5 to 1.5
- dt_bias: float32 [2, 48], P('section'), may hold values from -4 to -1
- a_log: float32 [2, 48], P('section'), may hold values from -10 to -1
- skip_d: float32 [2, 48], P('section'), may hold values from 0.5 to 1.5
- gate_gain: bfloat16 [2, 3072], P('section', 'dp'), may hold values from 0.5 to 1.5
- w_out: bfloat16 [2, 3072, 1536], P('section', None, 'dp'), may hold values from -0.109375 to 0.109375
Outputs:
- section_out: bfloat16 [2, 2, 8192, 1536], P('section', None, 'dp')
- in_grad: float32 [2, 2, 8192, 1536], P('section', None, 'dp')
- norm_gain_grad: float32 [2, 1536], P('section', 'dp')
- w_in_grad: float32 [2, 1536, 6448], P('section', 'dp')
- conv_weight_grad: float32 [2, 4, 3328], P('section', None, 'dp')
- conv_bias_grad: float32 [2, 3328], P('section', 'dp')
- dt_bias_grad: float32 [2, 48], P('section')
- a_log_grad: float32 [2, 48], P('section')
- skip_d_grad: float32 [2, 48], P('section')
- gate_gain_grad: float32 [2, 3072], P('section', 'dp')
- w_out_grad: float32 [2, 3072, 1536], P('section', None, 'dp')
Inputs may be any that keep to these rules, and one draw needn't show every extreme that they name: starts[m, d, 0] is 0 and each row never falls. In every micro-batch one device, drawn from the seed, holds a single sequence: its other entries are 128; on the other devices the 4 entries are distinct and below 128.
All inputs are finite; a program needn't handle non-finite values.
Results may differ from a plain program's by a relative error of at most 0.018.
Values may be sent and summed in bfloat16 or wider, within the bound.
A program may use at most 320 MiB of HBM per device.

v0:
```python
import jax
import jax.numpy as jnp
from jax import lax
from jax.experimental import pallas as pl
from jax.experimental.pallas import tpu as pltpu
from jax.sharding import Mesh, PartitionSpec as P

EPS = 1e-05
BF = jnp.bfloat16
F32 = jnp.float32
HIGH = lax.Precision.HIGHEST
D = 1536
CIN = 1152
HC = 384
NH = 6
RT = 1024
PK0 = 7
PKN = 14
HEAD0 = RT + 32
HALF = 768
ANY = pl.BlockSpec(memory_space=pl.ANY)
VM = pl.BlockSpec(memory_space=pltpu.VMEM)
SM = pl.BlockSpec(memory_space=pltpu.SMEM)
VLIM = 56 * 1024 * 1024


class Net:
    def __init__(self, ssem, rsem):
        self.ssem, self.rsem, self.n, self.all = ssem, rsem, 0, []

    def send(self, src, dst, dev):
        i = self.n
        self.n += 1
        assert i < self.ssem.shape[0]
        copy = pltpu.make_async_remote_copy(
            src_ref=src,
            dst_ref=dst,
            send_sem=self.ssem.at[i],
            recv_sem=self.rsem.at[i],
            device_id=dev,
            device_id_type=pl.DeviceIdType.MESH,
        )
        copy.start()
        self.all.append(copy)
        return copy

    def finish(self):
        for copy in self.all:
            copy.wait_send()


def place():
    s, z, h, x, c = (lax.axis_index(a) for a in ("s", "z", "h", "x", "c"))
    return s, z, h, x, c


def ring(i):
    return lax.rem(i + 1, 4), lax.rem(i + 3, 4), lax.rem(i + 2, 4)


def greet(devs):
    barrier = pltpu.get_barrier_semaphore()
    for dev in devs:
        pl.semaphore_signal(barrier, inc=1, device_id=dev, device_id_type=pl.DeviceIdType.MESH)
    pl.semaphore_wait(barrier, len(devs))


def zx_devs():
    s, z, h, x, c = place()
    zr, zl, _ = ring(z)
    xr, xl, _ = ring(x)
    return [{"z": zr}, {"z": zl}, {"x": xr}, {"x": xl}]


def ydev(y):
    return {"h": y // 2, "s": lax.rem(y, 2)}


def y_devs():
    s, z, h, x, c = place()
    yr, yl, _ = ring(2 * h + s)
    return [ydev(yr), ydev(yl), {"c": 1 - c}]


def group_devs():
    s, z, h, x, c = place()
    out = []
    for k in range(1, 8):
        out.append(
            {
                "s": 1 - s if k & 4 else s,
                "h": 1 - h if k & 2 else h,
                "c": 1 - c if k & 1 else c,
            }
        )
    return out


LAT = 1.7


def inter(gens):
    gens = [[0.0, g] for g in gens]
    while gens:
        item = min(gens, key=lambda v: v[0])
        if item[0] > 0:
            yield item[0]
        try:
            item[0] = next(item[1])
        except StopIteration:
            gens.remove(item)


def run(gens):
    for _ in inter(gens):
        pass


def g_ag_part(net, blk, out, local, i, axis_i, j, axis_j, pick, lanes, times):
    ir, il, io = ring(i)
    jr, jl, jo = ring(j)
    right, left = {axis_i: ir}, {axis_i: il}
    every = slice(None)

    def at(i, j, p):
        return out.at[pick(i, j, p) + (every, lanes)]

    own = blk.at[:, :, lanes]
    a1r = net.send(own, at(i, j, every), right)
    a1l = net.send(own, at(i, j, every), left)
    yield times[0]
    a1r.wait_recv()
    r = at(il, j, 0)
    a2r = net.send(r, r, right)
    a1l.wait_recv()
    r = at(ir, j, 1)
    a2l = net.send(r, r, left)
    yield times[1]
    a2r.wait_recv()
    a2l.wait_recv()
    local.wait()
    right, left = {axis_j: jr}, {axis_j: jl}
    r = at(every, j, every)
    a3r = net.send(r, r, right)
    a3l = net.send(r, r, left)
    yield times[2]
    a3r.wait_recv()
    r = at(every, jl, 0)
    a4r = net.send(r, r, right)
    a3l.wait_recv()
    r = at(every, jr, 1)
    a4l = net.send(r, r, left)
    yield times[3]
    a4r.wait_recv()
    a4l.wait_recv()


class Once:
    def __init__(self, copy):
        self.copy, self.open = copy, True
        copy.start()

    def wait(self):
        if self.open:
            self.copy.wait()
        self.open = False


def g_ag(net, blk, out, lsem, t0=0.0):
    s, z, h, x, c = place()
    local = Once(pltpu.make_async_copy(blk, out.at[z, :, x], lsem))
    q = HALF // 2
    gens = []
    for k in range(2):
        times = [t0 + v for v in ((3.4, 6.0, 13.8, 24.0) if k == 0 else (5.2, 7.0, 20.8, 28.0))]
        gens.append(
            g_ag_part(
                net, blk, out, local, x, "x", z, "z", lambda i, j, p: (j, p, i), pl.ds(k * q, q), times
            )
        )
        gens.append(
            g_ag_part(
                net,
                blk,
                out,
                local,
                z,
                "z",
                x,
                "x",
                lambda i, j, p: (i, p, j),
                pl.ds(HALF + k * q, q),
                times,
            )
        )
    yield from inter(gens)


def g_pairs(net, own, out, lsem, t0):
    s, z, h, x, c = place()
    outer, inner, sib = {"h": 1 - h, "s": 1 - s}, {"s": 1 - s}, {"c": 1 - c}
    first = []
    for k in range(2):
        rows = pl.ds(64 * k, 64)
        first.append(net.send(own.at[s, rows], out.at[h, c, s, rows], outer))
    local = pltpu.make_async_copy(own, out.at[h, c], lsem)
    local.start()
    c0 = net.send(own, out.at[h, c], sib)
    yield t0 + 4.6 + LAT
    second = []
    for k in range(2):
        first[k].wait_recv()
        r = out.at[1 - h, c, 1 - s, pl.ds(64 * k, 64)]
        second.append(net.send(r, r, inner))
        if k == 0:
            yield t0 + 9.2 + LAT
    r = out.at[1 - h, c, 1 - s]
    c1 = net.send(r, r, sib)
    yield t0 + 14 + LAT
    for copy in second:
        copy.wait_recv()
    r = out.at[1 - h, c, s]
    c2 = net.send(r, r, sib)
    yield t0 + 16 + LAT
    for copy in (c0, c1, c2):
        copy.wait_recv()
    local.wait()


NSUB = 4
SUBT = 9.25 / NSUB
ROWS = 128 // NSUB
PART = ROWS // 2


def g_yag(net, own, out, lsem, sub, t0=0.0):
    s, z, h, x, c = place()
    y = 2 * h + s
    yr, yl, yo = ring(y)
    rows = pl.ds(sub * ROWS, ROWS)
    lo, hi = pl.ds(sub * ROWS, PART), pl.ds(sub * ROWS + PART, PART)
    own = own.at[rows]
    mine = out.at[h, c, s, rows]
    local = pltpu.make_async_copy(own, mine, lsem)
    local.start()
    sib = {"c": 1 - c}
    c0 = net.send(own, mine, ydev(yr))
    c1 = net.send(own, mine, ydev(yl))
    c2 = net.send(own, mine, sib)
    t0 = t0 + 3 + (1.5 * NSUB + 1.5 * sub + 1) * SUBT + LAT
    yield t0
    c0.wait_recv()
    left = out.at[yl // 2, c, lax.rem(yl, 2)]
    c3 = net.send(left.at[lo], left.at[lo], ydev(yr))
    c4 = net.send(left.at[rows], left.at[rows], sib)
    c1.wait_recv()
    right = out.at[yr // 2, c, lax.rem(yr, 2)]
    c5 = net.send(right.at[hi], right.at[hi], ydev(yl))
    c6 = net.send(right.at[rows], right.at[rows], sib)
    yield t0 + SUBT + LAT
    c3.wait_recv()
    c5.wait_recv()
    far = out.at[yo // 2, c, lax.rem(yo, 2), rows]
    c7 = net.send(far, far, sib)
    yield t0 + SUBT + LAT + 2.5
    for copy in (c2, c4, c6, c7):
        copy.wait_recv()
    local.wait()


def xrs_scratch():
    return [
        pltpu.VMEM((4, 128, D), BF),
        pltpu.VMEM((4, 128, D), BF),
        pltpu.VMEM((2, NSUB, PART, D), BF),
        pltpu.VMEM((2, 128, D), BF),
    ]


def g_xrs(net, part, bufs, done, sub, t0=0.0):
    cb, sb, b1, b2 = bufs
    s, z, h, x, c = place()
    y = 2 * h + s
    yr, yl, yo = ring(y)
    sib = {"c": 1 - c}
    rows = pl.ds(sub * ROWS, ROWS)
    lo, hi = pl.ds(sub * ROWS, PART), pl.ds(sub * ROWS + PART, PART)
    units = [(k // 2, lax.rem(k, 2)) for k in (yo, yr, yl, y)]
    core = [
        net.send(part.at[units[k][0], 1 - c, units[k][1], rows], cb.at[k, rows], sib)
        for k in range(4)
    ]
    yield t0 + 2 + 4.4 / NSUB * sub

    def add(k):
        core[k].wait_recv()
        sb[k, rows] = (
            part[units[k][0], c, units[k][1], rows].astype(F32) + cb[k, rows].astype(F32)
        ).astype(BF)

    add(0)
    f0 = net.send(sb.at[0, lo], b1.at[0, sub], ydev(yr))
    f1 = net.send(sb.at[0, hi], b1.at[1, sub], ydev(yl))
    add(1)
    g1 = net.send(sb.at[1, hi], b2.at[0, hi], ydev(yr))
    add(2)
    g2 = net.send(sb.at[2, lo], b2.at[1, lo], ydev(yl))
    yield t0 + 3 + (1.5 * sub + 0.5) * SUBT + LAT
    f0.wait_recv()
    sb[1, lo] = (sb[1, lo].astype(F32) + b1[0, sub].astype(F32)).astype(BF)
    g3 = net.send(sb.at[1, lo], b2.at[0, lo], ydev(yr))
    f1.wait_recv()
    sb[2, hi] = (sb[2, hi].astype(F32) + b1[1, sub].astype(F32)).astype(BF)
    g4 = net.send(sb.at[2, hi], b2.at[1, hi], ydev(yl))
    yield t0 + 3 + (1.5 * sub + 2) * SUBT + LAT
    core[3].wait_recv()
    for copy in (g1, g2, g3, g4):
        copy.wait_recv()
    total = part[h, c, s, rows].astype(F32) + cb[3, rows].astype(F32)
    done(rows, total + b2[0, rows].astype(F32) + b2[1, rows].astype(F32))


QCOL = HALF // 2


def rs_scratch():
    return [
        pltpu.VMEM((4, 2, 4, 48, QCOL), BF),
        pltpu.VMEM((4, 2, 2, 4, 48, QCOL), BF),
        pltpu.VMEM((4, 2, 4, 48, QCOL), BF),
        pltpu.VMEM((4, 2, 4, 48, QCOL), BF),
        pltpu.VMEM((4, 2, 48, QCOL), BF),
        pltpu.VMEM((4, 2, 2, 48, QCOL), BF),
        pltpu.VMEM((4, 2, 48, QCOL), BF),
    ]


def g_rs_part(net, unit, i, axis_i, j, axis_j, bufs, done, times):
    b1, b2, t, sums, b3, b4, t2 = bufs
    ir, il, io = ring(i)
    jr, jl, jo = ring(j)
    right, left = {axis_i: ir}, {axis_i: il}
    f0 = net.send(unit(io, 0), b1.at[0], right)
    f1 = net.send(unit(io, 1), b1.at[1], left)
    yield times[0]
    g0 = net.send(unit(ir, 1), b2.at[0, 1], right)
    g1 = net.send(unit(il, 0), b2.at[1, 0], left)
    yield times[1]
    f0.wait_recv()
    t[0] = (unit(ir, 0)[...].astype(F32) + b1[0].astype(F32)).astype(BF)
    g2 = net.send(t.at[0], b2.at[0, 0], right)
    f1.wait_recv()
    t[1] = (unit(il, 1)[...].astype(F32) + b1[1].astype(F32)).astype(BF)
    g3 = net.send(t.at[1], b2.at[1, 1], left)
    yield times[2]
    for copy in (g0, g1, g2, g3):
        copy.wait_recv()

    def total(p, k):
        return (
            unit(i, p)[k].astype(F32) + b2[0, p, k].astype(F32) + b2[1, p, k].astype(F32)
        )

    def put(p, k):
        sums[p, k] = total(p, k).astype(BF)

    right, left = {axis_j: jr}, {axis_j: jl}
    put(0, jo)
    f0 = net.send(sums.at[0, jo], b3.at[0], right)
    put(1, jo)
    f1 = net.send(sums.at[1, jo], b3.at[1], left)
    put(1, jr)
    g0 = net.send(sums.at[1, jr], b4.at[0, 1], right)
    put(0, jl)
    g1 = net.send(sums.at[0, jl], b4.at[1, 0], left)
    yield times[3]
    f0.wait_recv()
    t2[0] = (total(0, jr) + b3[0].astype(F32)).astype(BF)
    g2 = net.send(t2.at[0], b4.at[0, 0], right)
    f1.wait_recv()
    t2[1] = (total(1, jl) + b3[1].astype(F32)).astype(BF)
    g3 = net.send(t2.at[1], b4.at[1, 1], left)
    yield times[4]
    for copy in (g0, g1, g2, g3):
        copy.wait_recv()
    for p in range(2):
        done(p, total(p, j) + b4[0, p].astype(F32) + b4[1, p].astype(F32))


def g_rs(net, grads, out, bufs, t0=0.0):
    s, z, h, x, c = place()
    gens = []

    def one(k, first_z):
        times = [t0 + v for v in ((0.2, 5.2, 16.0, 19.5, 23.0) if k % 2 == 0 else (5.0, 8.7, 23.0, 26.0, 29.0))]
        lanes = pl.ds(k * QCOL, QCOL)
        own = [b.at[k] for b in bufs]

        def put(p, v):
            out[p, :, k * QCOL : (k + 1) * QCOL] = v.astype(BF)

        if first_z:
            unit = lambda i, p: grads.at[i, p, :, :, lanes]
            return g_rs_part(net, unit, z, "z", x, "x", own, put, times)
        unit = lambda i, p: grads.at[:, p, i, :, lanes]
        return g_rs_part(net, unit, x, "x", z, "z", own, put, times)

    return inter([one(0, True), one(2, False), one(1, True), one(3, False)])


def wgrad_scratch():
    return [
        pltpu.VMEM((1024, D), BF),
        pltpu.VMEM((1024, D), BF),
        pltpu.VMEM((1024, CIN), BF),
        pltpu.VMEM((1024, HC), BF),
        pltpu.VMEM((4, 2, 4, 48, D), BF),
        pltpu.SemaphoreType.DMA((4,)),
    ]


def g_wgrad(srcs, bufs, sem, t0=0.0):
    copies = [pltpu.make_async_copy(a, b, sem.at[k]) for k, (a, b) in enumerate(zip(srcs, bufs))]
    for copy in copies:
        copy.start()
    yield t0 + 2.0
    u, e, dproj, o, grads = bufs
    copies[0].wait()
    copies[2].wait()
    for k in range(4):
        rows = slice(384 * k, 384 * k + 384)
        grads[k, :, :, :, 0:CIN] = tn(u[:, rows], dproj[...]).astype(BF).reshape(2, 4, 48, CIN)
        if k == 0:
            copies[1].wait()
            copies[3].wait()
        grads[k, :, :, :, CIN:D] = tn(e[:, rows], o[...]).astype(BF).reshape(2, 4, 48, HC)
        yield t0 + 2.0 + 1.7 * (k + 1)


def g_stats(net, mine, total, sb):
    sends = [net.send(mine, sb.at[k], dev) for k, dev in enumerate(group_devs())]
    yield 4.0
    acc = mine[...]
    for k, copy in enumerate(sends):
        copy.wait_recv()
        acc = acc + sb[k]
    total[...] = acc


def g_small(net, mine, bz, bx, total, t0=0.0):
    s, z, h, x, c = place()
    sends = [net.send(mine, bz.at[z], {"z": lax.rem(z + k, 4)}) for k in range(1, 4)]
    bz[z] = mine[...]
    yield t0 + 4.0
    for copy in sends:
        copy.wait_recv()
    bx[x] = bz[0] + bz[1] + bz[2] + bz[3]
    r = bx.at[x]
    sends = [net.send(r, r, {"x": lax.rem(x + k, 4)}) for k in range(1, 4)]
    yield t0 + 10.0
    for copy in sends:
        copy.wait_recv()
    total[...] = bx[0] + bx[1] + bx[2] + bx[3]


def small_scratch():
    return [pltpu.VMEM((4, 8, 640), F32), pltpu.VMEM((4, 8, 640), F32)]


def small_devs():
    s, z, h, x, c = place()
    return [{"z": lax.rem(z + k, 4)} for k in range(1, 4)] + [
        {"x": lax.rem(x + k, 4)} for k in range(1, 4)
    ]


def g_share(net, sums, got, vec, heads):
    s, z, h, x, c = place()
    me = (2 * s + h) * 2 + c
    sends = []
    for dev in group_devs():
        sends.append(net.send(sums.at[dev["s"]], got.at[me], dev))
    got[me] = sums[s]
    yield 20.0
    for copy in sends:
        copy.wait_recv()
    vec[...] = jnp.zeros_like(vec)
    tail = jnp.zeros((5, 256), F32)
    for q in range(8):
        lanes = slice(q * HC, q * HC + HC)
        vec[0:5, lanes] = got[q, 0:5, 0:HC]
        vec[5:6, lanes] = got[q, 5:6, 0:HC]
        tail = tail + got[q, 0:5, HC:640]
        heads[q : q + 1, 0:256] = got[q, 5:6, HC:640]
        heads[q : q + 1, 256:640] = got[q, 6:7, 0:HC]
    vec[0:5, 3072:3328] = tail


def params(cid):
    return pltpu.CompilerParams(
        collective_id=cid, has_side_effects=True, vmem_limit_bytes=VLIM
    )


def sems(n):
    return [pltpu.SemaphoreType.DMA((n,)), pltpu.SemaphoreType.DMA((n,))]


GATHERED = jax.ShapeDtypeStruct((4, 2, 4, 48, D), BF)
CHUNKS = jax.ShapeDtypeStruct((2, 2, 2, 128, D), BF)
SMALL = jax.ShapeDtypeStruct((8, 640), F32)
CHUNK = jax.ShapeDtypeStruct((128, D), BF)


def first_gathers(blk, tok, cot):
    def kernel(blk, tok, cot, w, tall, call, lsem, ssem, rsem):
        greet(zx_devs() + y_devs())
        net = Net(ssem, rsem)
        run(
            [
                g_ag(net, blk, w, lsem.at[0]),
                g_pairs(net, tok, tall, lsem.at[1], 0.0),
                g_pairs(net, cot, call, lsem.at[2], 9.2),
            ]
        )
        net.finish()

    return pl.pallas_call(
        kernel,
        name="first_gathers",
        out_shape=(GATHERED, CHUNKS, CHUNKS),
        in_specs=[VM] * 3,
        out_specs=(ANY,) * 3,
        scratch_shapes=[pltpu.SemaphoreType.DMA((3,))] + sems(48),
        compiler_params=params(0),
    )(blk, tok, cot)


def row_to_col(row):
    i = lax.broadcasted_iota(jnp.int32, (128, 128), 0)
    j = lax.broadcasted_iota(jnp.int32, (128, 128), 1)
    return jnp.sum(jnp.where(i == j, row, 0.0), axis=1, keepdims=True)


def col_to_row(col):
    i = lax.broadcasted_iota(jnp.int32, (128, 128), 0)
    j = lax.broadcasted_iota(jnp.int32, (128, 128), 1)
    return jnp.sum(jnp.where(i == j, col, 0.0), axis=0, keepdims=True)


def own_scale(total):
    s, z, h, x, c = place()
    row = total[pl.ds((2 * h + c) * 2 + s, 1), :]
    return lax.rsqrt(row_to_col(row) * (1.0 / 3072) + EPS)


def fetch(src, dst, sem):
    copy = pltpu.make_async_copy(src, dst, sem)
    copy.start()
    return copy


def forward_sum(part, stat, tok, blk):
    def kernel(part, stat, tok, blk, xall, w, total, fin, xo, cb, sb, b1, b2, stb, lsem, ssem, rsem):
        greet(zx_devs() + group_devs())
        net = Net(ssem, rsem)
        s, z, h, x, c = place()
        own = Once(pltpu.make_async_copy(tok.at[s], xo, lsem.at[0]))

        def done(rows, v):
            own.wait()
            scale = own_scale(total)[rows.start : rows.start + rows.size]
            fin[rows] = (xo[rows].astype(F32) + scale * v).astype(BF)

        def chain(sub):
            yield from g_xrs(net, part, (cb, sb, b1, b2), done, sub)
            yield from g_yag(net, fin, xall, lsem.at[2 + sub], sub)

        run(
            [g_stats(net, stat, total, stb)]
            + [chain(sub) for sub in range(NSUB)]
            + [g_ag(net, blk, w, lsem.at[1])]
        )
        net.finish()

    return pl.pallas_call(
        kernel,
        name="forward_sum",
        out_shape=(CHUNKS, GATHERED, jax.ShapeDtypeStruct((8, 128), F32)),
        in_specs=[VM, VM, ANY, VM],
        out_specs=(ANY, ANY, VM),
        scratch_shapes=[pltpu.VMEM((128, D), BF), pltpu.VMEM((128, D), BF)]
        + xrs_scratch()
        + [pltpu.VMEM((7, 8, 128), F32), pltpu.SemaphoreType.DMA((2 + NSUB,))]
        + sems(39 + 18 * NSUB),
        compiler_params=params(1),
    )(part, stat, tok, blk)


def stats_sum(stat):
    def kernel(stat, total, stb, ssem, rsem):
        greet(group_devs())
        net = Net(ssem, rsem)
        run([g_stats(net, stat, total, stb)])
        net.finish()

    return pl.pallas_call(
        kernel,
        name="stats_sum",
        out_shape=jax.ShapeDtypeStruct((16, 128), F32),
        in_specs=[VM],
        out_specs=VM,
        scratch_shapes=[pltpu.VMEM((7, 16, 128), F32)] + sems(8),
        compiler_params=params(2),
    )(stat)


def norm_back(v, x, e, ng):
    xf = x.astype(F32)
    vg = v * ng[...]
    r = lax.rsqrt(jnp.mean(xf * xf, axis=-1, keepdims=True) + EPS)
    dot = jnp.mean(xf * vg, axis=-1, keepdims=True)
    return e.astype(F32) + r * vg - xf * (r * r * r * dot)


def backward_sum(part, xall, cot, ng, wsrc, small):
    def kernel(part, xall, cot, ng, u, e, dproj, o, small, eall, out, hsum, fin, xo, eo, *rest):
        cbs, bufs, wbufs, rest = rest[:4], rest[4:11], rest[11:17], rest[17:]
        bz, bx, lsem, ssem, rsem = rest
        greet(small_devs() + y_devs())
        net = Net(ssem, rsem)
        s, z, h, x, c = place()
        ox = Once(pltpu.make_async_copy(xall.at[h, c, s], xo, lsem.at[0]))
        oe = Once(pltpu.make_async_copy(cot.at[s], eo, lsem.at[1]))

        def done(rows, v):
            ox.wait()
            oe.wait()
            fin[rows] = norm_back(v, xo[rows], eo[rows], ng).astype(BF)

        def chain(sub):
            yield from g_xrs(net, part, cbs, done, sub)
            yield from g_yag(net, fin, eall, lsem.at[2 + sub], sub)

        def weights():
            yield from g_wgrad((u, e, dproj, o), wbufs[:5], wbufs[5])
            yield from g_rs(net, wbufs[4], out, bufs, 9.0)

        run(
            [chain(sub) for sub in range(NSUB)]
            + [weights(), g_small(net, small, bz, bx, hsum)]
        )
        net.finish()

    return pl.pallas_call(
        kernel,
        name="backward_sum",
        out_shape=(CHUNKS, jax.ShapeDtypeStruct((2, 48, D), BF), SMALL),
        in_specs=[VM, ANY, ANY, VM, ANY, ANY, ANY, ANY, VM],
        out_specs=(ANY, VM, VM),
        scratch_shapes=[pltpu.VMEM((128, D), BF)] * 3
        + xrs_scratch()
        + rs_scratch()
        + wgrad_scratch()
        + small_scratch()
        + [pltpu.SemaphoreType.DMA((2 + NSUB,))]
        + sems(54 + 18 * NSUB),
        compiler_params=params(3),
    )(part, xall, cot, ng, *wsrc, small)


def last_sums(part0, tok, eall, ng, part1, xall, stat1, wsrc, small0, small1):
    def kernel(p0, tok, eall, ng, p1, xall, st, u, e, dproj, o, sm0, sm1, ig, so, out, vec, heads, *rest):
        xo, eo, x1, ba, bb, rest = rest[0], rest[1], rest[2], rest[3:7], rest[7:11], rest[11:]
        bufs, wbufs, rest = rest[:7], rest[7:13], rest[13:]
        bz, bx, sums, got, lsem, ssem, rsem = rest
        greet(small_devs() + group_devs())
        net = Net(ssem, rsem)
        s, z, h, x, c = place()
        ox = Once(pltpu.make_async_copy(tok.at[s], xo, lsem.at[0]))
        oe = Once(pltpu.make_async_copy(eall.at[h, c, s], eo, lsem.at[1]))
        o1 = Once(pltpu.make_async_copy(xall.at[h, c, s], x1, lsem.at[2]))

        def done0(rows, v):
            ox.wait()
            oe.wait()
            ig[rows] = norm_back(v, xo[rows], eo[rows], ng).astype(BF)

        def done1(rows, v):
            o1.wait()
            scale = own_scale(st)[rows.start : rows.start + rows.size]
            so[rows] = (x1[rows].astype(F32) + scale * v).astype(BF)

        def weights():
            yield from g_wgrad((u, e, dproj, o), wbufs[:5], wbufs[5])
            yield from g_rs(net, wbufs[4], out, bufs, 9.0)

        def smalls():
            sums[1] = sm1[...]
            yield from g_small(net, sm0, bz, bx, sums.at[0])
            yield from g_share(net, sums, got, vec, heads)

        run(
            [g_xrs(net, p1, bb, done1, sub) for sub in range(NSUB)]
            + [g_xrs(net, p0, ba, done0, sub) for sub in range(NSUB)]
            + [weights(), smalls()]
        )
        net.finish()

    return pl.pallas_call(
        kernel,
        name="last_sums",
        out_shape=(
            CHUNK,
            CHUNK,
            jax.ShapeDtypeStruct((2, 48, D), BF),
            jax.ShapeDtypeStruct((8, 3328), F32),
            SMALL,
        ),
        in_specs=[VM, ANY, ANY, VM, VM, ANY, VM, ANY, ANY, ANY, ANY, VM, VM],
        out_specs=(VM,) * 5,
        scratch_shapes=[pltpu.VMEM((128, D), BF)] * 3
        + xrs_scratch()
        + xrs_scratch()
        + rs_scratch()
        + wgrad_scratch()
        + small_scratch()
        + [pltpu.VMEM((2, 8, 640), F32), pltpu.VMEM((8, 8, 640), F32)]
        + [pltpu.SemaphoreType.DMA((3,))]
        + sems(61 + 20 * NSUB),
        compiler_params=params(4),
    )(part0, tok, eall, ng, part1, xall, stat1, *wsrc, small0, small1)


def nt(a, b):
    return lax.dot_general(a, b, (((1,), (1,)), ((), ())), preferred_element_type=F32)


def tn(a, b):
    return lax.dot_general(a, b, (((0,), (0,)), ((), ())), preferred_element_type=F32)


def iotas():
    i = lax.broadcasted_iota(jnp.int32, (128, 128), 0)
    j = lax.broadcasted_iota(jnp.int32, (128, 128), 1)
    return i, j


def seg_of(st, chunk, places):
    seg = jnp.full(places.shape, -1, jnp.int32)
    for k in range(4):
        seg = seg + (st[chunk, k] <= places).astype(jnp.int32)
    return seg


def masks(st, chunk):
    i, j = iotas()
    seg = seg_of(st, chunk, i)
    keep = jnp.logical_and(seg == seg_of(st, chunk, j), i >= j)
    valid = [None] + [
        (seg_of(st, chunk, i - k) == seg).astype(F32) for k in range(1, 4)
    ]
    return keep, valid


def conv_tile(xt, cv, t, valid):
    lanes = slice(128 * t, 128 * t + 128)
    pre = cv[4:5, lanes] + cv[3:4, lanes] * xt
    moved = [xt]
    for k in range(1, 4):
        m = pltpu.roll(xt, k, axis=0) * valid[k]
        moved.append(m)
        pre = pre + cv[3 - k : 4 - k, lanes] * m
    return pre, moved


def rates(rt, cv):
    i, j = iotas()
    head = j < NH
    v = rt + cv[7:8, 0:128]
    dt = jnp.where(head, jnp.maximum(v, 0.0) + jnp.log1p(jnp.exp(-jnp.abs(v))), 0.0)
    lower = (i >= j).astype(F32)
    cum = jnp.dot(
        lower, -dt * cv[8:9, 0:128], precision=HIGH, preferred_element_type=F32
    )
    return v, dt, cum


def half_masks():
    _, j = iotas()
    return j < 64


def split_pair(v, low):
    zero = jnp.zeros_like(v)
    return jnp.concatenate([jnp.where(low, v, zero), jnp.where(low, zero, v)], axis=0)


def decay_of(keep, cum, cum_t, h):
    spread = jnp.where(keep, cum[:, h : h + 1] - cum_t[h : h + 1, :], -1e30)
    return jnp.exp(spread)


def load_const(cv):
    return cv[...]


def front(xb, w, ng, u_out):
    xf = xb[...].astype(F32)
    r = lax.rsqrt(jnp.mean(xf * xf, axis=-1, keepdims=True) + EPS)
    u = (xf * r * ng[...]).astype(BF)
    u_out[...] = u
    return jnp.dot(u, w[:, 0:CIN], preferred_element_type=F32)


def make_forward(with_do):
    def kernel(st, x, w, ng, cv, *rest):
        if with_do:
            e, part, stat, proj, yout, uout, doo, og = rest
        else:
            part, stat, proj, yout, uout, og = rest
        step = pl.program_id(0)
        proj[...] = front(x, w, ng, uout)
        if with_do:
            doo[...] = jnp.dot(e[...], w[:, CIN:D], preferred_element_type=F32)
        low = half_masks()
        for m in range(2):
            rows = slice(128 * m, 128 * m + 128)
            chunk = step * 2 + m
            keep, valid = masks(st, chunk)
            act = []
            for t in range(5):
                pre, _ = conv_tile(proj[rows, HC + 128 * t : HC + 128 * t + 128], cv, t, valid)
                act.append((pre * jax.nn.sigmoid(pre)).astype(BF))
            _, dt, cum = rates(proj[rows, RT:CIN], cv)
            cum_t, dt_t = jnp.transpose(cum), jnp.transpose(dt)
            gram = nt(act[4], act[3])
            gsum = jnp.zeros((128, 1), F32)
            tsum = jnp.zeros((128, 1), F32)
            for t in range(3):
                lanes = slice(128 * t, 128 * t + 128)
                mixes = []
                for h in (2 * t, 2 * t + 1):
                    dec = decay_of(keep, cum, cum_t, h)
                    mixes.append((gram * dec * dt_t[h : h + 1, :]).astype(BF))
                y = jnp.dot(
                    jnp.concatenate(mixes, axis=1),
                    split_pair(act[t], low),
                    preferred_element_type=F32,
                )
                y = y + cv[6:7, lanes] * act[t].astype(F32)
                yout[rows, lanes] = y
                zt = proj[rows, lanes]
                g = y * (zt * jax.nn.sigmoid(zt))
                gsum = gsum + jnp.sum(g * g, axis=1, keepdims=True)
                gain = cv[5:6, lanes]
                og[rows, lanes] = (g * gain).astype(BF)
                if with_do:
                    tsum = tsum + jnp.sum(g * gain * doo[rows, lanes], axis=1, keepdims=True)
            stat[pl.ds(chunk, 1), :] = col_to_row(gsum)
            if with_do:
                stat[pl.ds(chunk + 8, 1), :] = col_to_row(tsum)
        part[...] = nt(og[...], w[:, CIN:D]).astype(BF)

    return kernel


def rows_spec(cols):
    return pl.BlockSpec((256, cols), lambda i: (i, 0))


def whole(*shape):
    return pl.BlockSpec(shape, lambda i: (0,) * len(shape))


def layer_forward(st, x, w, ng, cv, e=None):
    with_do = e is not None
    n_stat = 16 if with_do else 8
    ins = [st, x, w, ng, cv] + ([e] if with_do else [])
    in_specs = [SM, rows_spec(D), whole(D, D), whole(1, D), whole(16, 640)] + (
        [rows_spec(D)] if with_do else []
    )
    outs = [
        jax.ShapeDtypeStruct((1024, D), BF),
        jax.ShapeDtypeStruct((n_stat, 128), F32),
        jax.ShapeDtypeStruct((1024, CIN), F32),
        jax.ShapeDtypeStruct((1024, HC), F32),
        jax.ShapeDtypeStruct((1024, D), BF),
    ] + ([jax.ShapeDtypeStruct((1024, HC), F32)] if with_do else [])
    out_specs = [
        rows_spec(D),
        whole(n_stat, 128),
        rows_spec(CIN),
        rows_spec(HC),
        rows_spec(D),
    ] + ([rows_spec(HC)] if with_do else [])
    return pl.pallas_call(
        make_forward(with_do),
        name="layer_forward",
        grid=(4,),
        in_specs=in_specs,
        out_specs=out_specs,
        out_shape=outs,
        scratch_shapes=[pltpu.VMEM((256, HC), BF)],
        compiler_params=pltpu.CompilerParams(vmem_limit_bytes=VLIM),
    )(*ins)


def make_backward(first):
    def kernel(st, e, w, cv, proj, yin, stat, *rest):
        if first:
            x, x1, dproj, oo, part, sm, do = rest
        else:
            do, dproj, oo, part, sm = rest
        step = pl.program_id(0)

        @pl.when(step == 0)
        def _():
            sm[...] = jnp.zeros_like(sm)

        if first:
            do[...] = jnp.dot(e[...], w[:, CIN:D], preferred_element_type=F32)
        low = half_masks()
        i, j = iotas()
        upper = (j >= i).astype(F32)

        def add(row, lanes, v):
            sm[row : row + 1, lanes] += jnp.sum(v, axis=0, keepdims=True)

        for m in range(2):
            rows = slice(128 * m, 128 * m + 128)
            chunk = step * 2 + m
            keep, valid = masks(st, chunk)
            pres, moves, act = [], [], []
            for t in range(5):
                pre, moved = conv_tile(
                    proj[rows, HC + 128 * t : HC + 128 * t + 128], cv, t, valid
                )
                pres.append(pre)
                moves.append(moved)
                act.append((pre * jax.nn.sigmoid(pre)).astype(BF))
            v, dt, cum = rates(proj[rows, RT:CIN], cv)
            cum_t, dt_t = jnp.transpose(cum), jnp.transpose(dt)
            gram = nt(act[4], act[3])
            r = lax.rsqrt(row_to_col(stat[pl.ds(chunk, 1), :]) * (1.0 / 3072) + EPS)
            if first:
                dots = jnp.sum(
                    e[rows, :].astype(F32) * (x1[rows, :].astype(F32) - x[rows, :].astype(F32)),
                    axis=1,
                    keepdims=True,
                )
                k = r * r * dots * (1.0 / 3072)
            else:
                k = r * r * r * row_to_col(stat[pl.ds(chunk + 8, 1), :]) * (1.0 / 3072)
            dact = []
            dgram = jnp.zeros((128, 128), F32)
            dcum = jnp.zeros((128, 128), F32)
            col_rows = []
            for t in range(3):
                lanes = slice(128 * t, 128 * t + 128)
                zt, y, dot_ = proj[rows, lanes], yin[rows, lanes], do[rows, lanes]
                gain = cv[5:6, lanes]
                sig = jax.nn.sigmoid(zt)
                sz = zt * sig
                g = y * sz
                oo[rows, lanes] = (g * r * gain).astype(BF)
                add(5, lanes, dot_ * g * r)
                dg = r * (dot_ * gain) - g * k
                dproj[rows, lanes] = (dg * y * (sig + sz * (1.0 - sig))).astype(BF)
                dy = (dg * sz).astype(BF)
                dyf = dy.astype(F32)
                xs = act[t]
                add(6, lanes, dyf * xs.astype(F32))
                dy2 = split_pair(dy, low)
                dmix2 = nt(dy2, xs)
                mixes = []
                for q in range(2):
                    h = 2 * t + q
                    dec = decay_of(keep, cum, cum_t, h)
                    dt_row = dt_t[h : h + 1, :]
                    pm = gram * dec
                    mixes.append((pm * dt_row).astype(BF))
                    dmix = dmix2[128 * q : 128 * q + 128]
                    dgram = dgram + dmix * (dec * dt_row)
                    vm = dmix * pm
                    col_rows.append(jnp.sum(vm, axis=0, keepdims=True))
                    rsum = jnp.sum(vm * dt_row, axis=1, keepdims=True)
                    dcum = dcum + jnp.where(j == h, rsum, 0.0)
                dxs = tn(jnp.concatenate(mixes, axis=0), dy2)
                dact.append(dxs + cv[6:7, lanes] * dyf)
            dgl = dgram.astype(BF)
            dact.append(tn(dgl, act[4]))
            dact.append(jnp.dot(dgl, act[3], preferred_element_type=F32))
            ddt = jnp.transpose(
                jnp.concatenate(col_rows + [jnp.zeros((128 - NH, 128), F32)], axis=0)
            )
            dcum = dcum - ddt * dt
            dla = jnp.dot(upper, dcum, precision=HIGH, preferred_element_type=F32)
            nexp = -cv[8:9, 0:128]
            drate = (ddt + dla * nexp) * jax.nn.sigmoid(v)
            drate = jnp.where(j < NH, drate, 0.0)
            add(5, slice(HC, HC + 128), drate)
            add(5, slice(HC + 128, 640), dla * dt * nexp)
            dproj[rows, RT:CIN] = drate.astype(BF)
            for t in range(5):
                lanes = slice(128 * t, 128 * t + 128)
                pre = pres[t]
                sp = jax.nn.sigmoid(pre)
                dpre = dact[t] * (sp + pre * sp * (1.0 - sp))
                add(4, lanes, dpre)
                add(3, lanes, dpre * moves[t][0])
                dx = cv[3:4, lanes] * dpre
                for n in range(1, 4):
                    add(3 - n, lanes, dpre * moves[t][n])
                    dx = dx + cv[3 - n : 4 - n, lanes] * pltpu.roll(
                        dpre * valid[n], 128 - n, axis=0
                    )
                dproj[rows, HC + 128 * t : HC + 128 * t + 128] = dx.astype(BF)
        part[...] = nt(dproj[...], w[:, 0:CIN]).astype(BF)

    return kernel


def layer_backward(st, e, w, cv, proj, y, stat, do=None, x=None, x1=None):
    first = do is None
    extra = [x, x1] if first else [do]
    ins = [st, e, w, cv, proj, y, stat] + extra
    in_specs = [
        SM,
        rows_spec(D),
        whole(D, D),
        whole(16, 640),
        rows_spec(CIN),
        rows_spec(HC),
        whole(*stat.shape),
    ] + ([rows_spec(D), rows_spec(D)] if first else [rows_spec(HC)])
    outs = [
        jax.ShapeDtypeStruct((1024, CIN), BF),
        jax.ShapeDtypeStruct((1024, HC), BF),
        jax.ShapeDtypeStruct((1024, D), BF),
        SMALL,
    ]
    return pl.pallas_call(
        make_backward(first),
        name="layer_backward",
        grid=(4,),
        in_specs=in_specs,
        out_specs=[rows_spec(CIN), rows_spec(HC), rows_spec(D), whole(8, 640)],
        out_shape=outs,
        scratch_shapes=[pltpu.VMEM((256, HC), F32)] if first else [],
        compiler_params=pltpu.CompilerParams(vmem_limit_bytes=VLIM),
    )(*ins)


def pack_shards(starts, norm_gain, w_in, conv_weight, conv_bias, gate_gain, w_out):
    small = jnp.concatenate(
        [
            conv_weight.reshape(-1),
            conv_bias,
            gate_gain,
            starts.reshape(-1).astype(BF),
            jnp.zeros((20,), BF),
        ]
    ).reshape(24, PKN)
    wide = jnp.concatenate([norm_gain[:, None], small], axis=1)

    def each(v):
        return jnp.broadcast_to(v[:, None], (24, 8, v.shape[-1]))

    rate = jnp.concatenate(
        [w_in[:, 6400:].reshape(24, 8, NH), each(wide), jnp.zeros((24, 8, 107), BF)], axis=-1
    )
    pieces = jnp.concatenate(
        [
            w_in[:, :3072].reshape(24, 8, HC),
            w_in[:, 3072:6144].reshape(24, 8, HC),
            each(w_in[:, 6144:6400]),
            rate,
            jnp.transpose(w_out).reshape(24, 8, HC),
        ],
        axis=-1,
    )
    return jnp.transpose(pieces, (1, 0, 2))


def constants(w, q, dt_bias, a_log, skip_d):
    tile = w[:, RT : RT + 128].astype(F32)
    pairs = jnp.transpose(tile[:, NH : NH + 2 * (PKN + 1)].reshape(D, 2, PKN + 1), (1, 0, 2))
    ng = pairs[:, None, :, 0]
    small = pairs[:, :, 1:].reshape(2, 64, 24 * PKN)
    taps = jnp.transpose(small[:, :, :208].reshape(2, 64, 4, 52), (0, 2, 1, 3)).reshape(2, 4, 3328)
    conv = jnp.concatenate([taps, small[:, :, 208:260].reshape(2, 1, 3328)], axis=1)
    gate = small[:, :, 260:308].reshape(2, 1, 3072)
    conv = jnp.concatenate(
        [lax.dynamic_slice_in_dim(conv, q * HC, HC, 2), conv[:, :, 3072:]], axis=2
    )
    gate = lax.dynamic_slice_in_dim(gate, q * HC, HC, 2)

    def heads(v):
        return lax.dynamic_slice_in_dim(v, q * NH, NH, 1)

    skip = jnp.repeat(heads(skip_d), 64, axis=1)[:, None]
    pad = lambda v: jnp.pad(v, ((0, 0), (0, 0), (0, 640 - v.shape[2])))
    rows = [
        conv,
        pad(gate),
        pad(skip),
        pad(heads(dt_bias)[:, None]),
        pad(heads(jnp.exp(a_log))[:, None]),
        jnp.zeros((2, 7, 640), F32),
    ]
    return jnp.concatenate(rows, axis=1), ng


def unpack_grads(rec, vec, heads, w_in, norm_gain, place_dp):
    rec = rec.astype(F32)
    flat = lambda v: jnp.transpose(v, (1, 0, 2)).reshape(24, -1)
    w_in_grad = jnp.concatenate(
        [
            flat(rec[:, :, 0:HC]),
            flat(rec[:, :, HC : 2 * HC]),
            jnp.sum(rec[:, :, 2 * HC : RT], axis=0),
            flat(rec[:, :, RT : RT + NH]),
        ],
        axis=1,
    )
    w_out_grad = jnp.transpose(flat(rec[:, :, CIN:D]))
    conv = lax.dynamic_slice_in_dim(vec[0:5], 52 * place_dp, 52, 1)
    gate = lax.dynamic_slice_in_dim(vec[5], 48 * place_dp, 48, 0)
    norm_grad = jnp.sum(w_in.astype(F32) * w_in_grad, axis=1) / norm_gain.astype(F32)
    return (
        norm_grad,
        w_in_grad,
        conv[0:4],
        conv[4],
        heads[:, 0:NH].reshape(48),
        heads[:, 128 : 128 + NH].reshape(48),
        jnp.sum(heads[:, 256:640].reshape(48, 64), axis=1),
        gate,
        w_out_grad,
    )


GROUP = ("s", "h", "c")


def body(
    tokens,
    cotangent,
    starts,
    norm_gain,
    w_in,
    conv_weight,
    conv_bias,
    dt_bias,
    a_log,
    skip_d,
    gate_gain,
    w_out,
):
    s, z, h, x, c = place()
    q = (s * 2 + h) * 2 + c
    mine = pack_shards(
        starts[:, 0], norm_gain[0], w_in[0], conv_weight[0], conv_bias[0], gate_gain[0], w_out[0]
    )
    rec = lax.all_to_all(mine, GROUP, 0, 0, tiled=True)
    blocks = rec.reshape(2, 2, 48, D)
    st = (
        rec[0:4, :, RT + PK0 : RT + PK0 + PKN]
        .reshape(4, 24 * PKN)[:, 308:316]
        .reshape(8, 4)
        .astype(jnp.int32)
    )
    gap = lambda v, n: jnp.pad(v, ((0, 0), (0, 0), (n, D - n - v.shape[2])))
    blk0 = blocks[0] + gap(blocks[1, :, :, RT + NH : RT + PK0 + PKN], RT + PK0 + PKN)
    heads = jnp.stack([dt_bias[0], a_log[0], skip_d[0]])
    other = lax.ppermute(heads, "s", [(0, 1), (1, 0)])
    heads = jnp.where(s == 0, jnp.stack([heads, other]), jnp.stack([other, heads]))

    w0, tall, call = first_gathers(blk0, tokens, cotangent)
    w0 = w0.reshape(D, D)
    x0 = tall.reshape(1024, D)
    e1 = call.reshape(1024, D)
    cv, ng = constants(w0, q, heads[:, 0], heads[:, 1], heads[:, 2])
    part, stat0, proj0, y0, u0 = layer_forward(st, x0, w0, ng[0], cv[0])
    xall, w1, stat0 = forward_sum(part.reshape(2, 2, 2, 128, D), stat0, tokens, blocks[1])
    w1 = w1.reshape(D, D)
    x1 = xall.reshape(1024, D)
    part1, stat1, proj1, y1, u1, do1 = layer_forward(st, x1, w1, ng[1], cv[1], e1)
    stat1 = stats_sum(stat1)
    dproj1, o1, dpart1, sm1 = layer_backward(st, e1, w1, cv[1], proj1, y1, stat1, do=do1)
    eall, gs1, sm1 = backward_sum(
        dpart1.reshape(2, 2, 2, 128, D), xall, cotangent, ng[1], (u1, e1, dproj1, o1), sm1
    )
    e0 = eall.reshape(1024, D)
    dproj0, o0, dpart0, sm0 = layer_backward(st, e0, w0, cv[0], proj0, y0, stat0, x=x0, x1=x1)
    ig0, so1, gs0, vec, hd = last_sums(
        dpart0.reshape(2, 2, 2, 128, D),
        tokens,
        eall,
        ng[0],
        part1.reshape(2, 2, 2, 128, D),
        xall,
        stat1[0:8],
        (u0, e0, dproj0, o0),
        sm0,
        sm1,
    )
    back = lax.all_to_all(jnp.stack([gs0, gs1]).reshape(8, 24, D), GROUP, 0, 0, tiled=True)
    place_dp = ((z * 2 + h) * 4 + x) * 2 + c
    outs = unpack_grads(back, vec, hd, w_in[0], norm_gain[0], place_dp)

    got = lax.ppermute(jnp.where(s == 0, so1, ig0), "s", [(0, 1), (1, 0)])
    ig = jnp.where(s == 0, jnp.stack([ig0, got]), eall[h, c])
    so = jnp.where(s == 0, xall[h, c], jnp.stack([got, so1]))
    return (so[None], ig.astype(F32)[None]) + tuple(o[None] for o in outs)


def solution(mesh):
    inner = Mesh(mesh.devices.reshape(2, 4, 2, 4, 2), ("s", "z", "h", "x", "c"))
    dp = ("z", "h", "x", "c")
    in_specs = (
        P(None, dp, None),
        P(None, dp, None),
        P(None, dp, None),
        P("s", dp),
        P("s", dp, None),
        P("s", None, dp),
        P("s", dp),
        P("s", None),
        P("s", None),
        P("s", None),
        P("s", dp),
        P("s", None, dp),
    )
    out_specs = (
        P("s", None, dp, None),
        P("s", None, dp, None),
        P("s", dp),
        P("s", dp, None),
        P("s", None, dp),
        P("s", dp),
        P("s", None),
        P("s", None),
        P("s", None),
        P("s", dp),
        P("s", None, dp),
    )
    return jax.shard_map(body, mesh=inner, in_specs=in_specs, out_specs=out_specs, check_vma=False)
```

profile of v0, /device:TPU:1, one launch (start us, length us, event | category | flops | bytes accessed | tf_op | source)
XLA Modules:
  0.0 354.1 jit_solution(6657034558498878807)
XLA Ops:
  0.7 1.0 fusion.7
  4.2 0.8 reshape_squeeze.4
  4.9 1.4 concatenate.35
  6.5 0.8 copy.87
  7.2 0.9 copy_bitcast_fusion
  8.3 1.0 concatenate.37
  9.3 6.0 %all-to-all-start = ((bf16[8,24,1536]{2,1,0:T(8,128)(2,1)}), bf16[8,24,1536]{2,1,0:T(8,128)(2,1)S(1)}, u32[]{:S(2)}, u32[]{:S(2)}) async-start(bf16[8,24,1536]{2,1,0:T(8,128)(2,1)} %bitcast.6), calls=%async_computation | async-start | bytes 1179648 | tf_op jit(solution)/shard_map/all_to_all | solution.py:1166
  15.3 1.5 collective-permute-start
  16.8 7.2 %collective-permute-done = f32[3,48]{1,0:T(4,128)S(1)} collective-permute-done((f32[3,48]{1,0:T(4,128)S(1)}, f32[3,48]{1,0:T(4,128)S(1)}, u32[]{:S(2)}, u32[]{:S(2)}) %collective-permute-start) | collective-permute-done | bytes 608 | tf_op jit(solution)/shard_map/ppermute | solution.py:1177
  24.6 0.8 fusion.6
  25.4 0.8 bitcast_add_fusion.blk
  26.2 36.5 %first_gathers.1 = (bf16[4,2,4,48,1536]{4,3,2,1,0:T(8,128)(2,1)}, bf16[2,2,2,128,1536]{4,3,2,1,0:T(8,128)(2,1)}, bf16[2,2,2,128,1536]{4,3,2,1,0:T(8,128)(2,1)}) custom-call(bf16[2,48,1536]{2,1,0:T(8,128)(2,1)} %bitcast_add_fusion.blk, bf16[2,128,1536]{2,1,0:T(8,128)(2,1)} %tok.5, bf16[2,128,1536]{2,1,0:T(8,128)(2,1)} %cot.3), custom_call_target="tpu_custom_call" | custom-call | tf_op jit(solution)/shard_map/first_gathers/pallas_call | solution.py:528
  62.7 1.2 slice_convert_fusion
  68.5 15.2 %layer_forward.2 = (bf16[1024,1536]{1,0:T(8,128)(2,1)}, f32[8,128]{1,0:T(8,128)}, f32[1024,1152]{1,0:T(8,128)}, f32[1024,384]{1,0:T(8,128)}, bf16[1024,1536]{1,0:T(8,128)(2,1)}) custom-call(s32[8,4]{1,0:T(8,128)} %reshape.241.st, bf16[1024,1536]{1,0:T(8,128)(2,1)} %bitcast.106, bf16[1536,1536]{1,0:T(8,128)(2,1)} %bitcast.102, ...), custom_call_target="tpu_custom_call" | custom-call | tf_op jit(solution)/shard_map/layer_forward/pallas_call | solution.py:897
  83.6 49.5 %forward_sum.1 = (bf16[2,2,2,128,1536]{4,3,2,1,0:T(8,128)(2,1)}, bf16[4,2,4,48,1536]{4,3,2,1,0:T(8,128)(2,1)}, f32[8,128]{1,0:T(8,128)}) custom-call(bf16[2,2,2,128,1536]{4,3,2,1,0:T(8,128)(2,1)} %bitcast.111, f32[8,128]{1,0:T(8,128)} %get-tuple-element.47.stat, bf16[2,128,1536]{2,1,0:T(8,128)(2,1)} %tok.5, bf16[2,48,1536]{2,1,0:T(8,128)(2,1)} %bitcast.118), custom_call_target="tpu_custom_call" | custom-call | tf_op jit(solution)/shard_map/forward_sum/pallas_call | solution.py:586
  133.1 16.4 %layer_forward.3 = (bf16[1024,1536]{1,0:T(8,128)(2,1)}, f32[16,128]{1,0:T(8,128)}, f32[1024,1152]{1,0:T(8,128)}, f32[1024,384]{1,0:T(8,128)}, bf16[1024,1536]{1,0:T(8,128)(2,1)}, /*index=5*/f32[1024,384]{1,0:T(8,128)}) custom-call(s32[8,4]{1,0:T(8,128)} %reshape.241.st, bf16[1024,1536]{1,0:T(8,128)(2,1)} %bitcast.94, bf16[1536,1536]{1,0:T(8,128)(2,1)} %bitcast.104, ...), custom_call_target="tpu_custom_call" | custom-call | tf_op jit(solution)/shard_map/layer_forward/pallas_call | solution.py:897
  149.5 7.8 %stats_sum.1.stat = f32[16,128]{1,0:T(8,128)} custom-call(f32[16,128]{1,0:T(8,128)} %get-tuple-element.53.stat), custom_call_target="tpu_custom_call" | custom-call | tf_op jit(solution)/shard_map/stats_sum/pallas_call | solution.py:607
  157.3 1.3 slice.141.st
  158.6 20.5 %layer_backward.2 = (bf16[1024,1152]{1,0:T(8,128)(2,1)}, bf16[1024,384]{1,0:T(8,128)(2,1)}, bf16[1024,1536]{1,0:T(8,128)(2,1)}, f32[8,640]{1,0:T(8,128)}) custom-call(s32[8,4]{1,0:T(8,128)} %reshape.241.st, bf16[1024,1536]{1,0:T(8,128)(2,1)} %bitcast.99, bf16[1536,1536]{1,0:T(8,128)(2,1)} %bitcast.105, f32[16,640]{1,0:T(8,128)} %get-tuple-element.90.cv, ...), custom_call_target="tpu_custom_call" | custom-call | tf_op jit(solution)/shard_map/layer_backward/pallas_call | solution.py:1043
  179.1 57.3 %backward_sum.1 = (bf16[2,2,2,128,1536]{4,3,2,1,0:T(8,128)(2,1)}, bf16[2,48,1536]{2,1,0:T(8,128)(2,1)}, f32[8,640]{1,0:T(8,128)}) custom-call(bf16[2,2,2,128,1536]{4,3,2,1,0:T(8,128)(2,1)} %bitcast.110, bf16[2,2,2,128,1536]{4,3,2,1,0:T(8,128)(2,1)} %get-tuple-element.48.xall, bf16[2,128,1536]{2,1,0:T(8,128)(2,1)} %cot.3, f32[1,1536]{1,0:T(1,128)} %get-tuple-element.88.ng, ...), custom_call_target="tpu_custom_call" | custom-call | tf_op jit(solution)/shard_map/backward_sum/pallas_call | solution.py:655
  236.4 23.7 %layer_backward.3 = (bf16[1024,1152]{1,0:T(8,128)(2,1)}, bf16[1024,384]{1,0:T(8,128)(2,1)}, bf16[1024,1536]{1,0:T(8,128)(2,1)}, f32[8,640]{1,0:T(8,128)}) custom-call(s32[8,4]{1,0:T(8,128)} %reshape.241.st, bf16[1024,1536]{1,0:T(8,128)(2,1)} %bitcast.96, bf16[1536,1536]{1,0:T(8,128)(2,1)} %bitcast.103, f32[16,640]{1,0:T(8,128)} %get-tuple-element.91.cv, ...), custom_call_target="tpu_custom_call" | custom-call | tf_op jit(solution)/shard_map/layer_backward/pallas_call | solution.py:1043
  260.1 56.0 %last_sums.1 = (bf16[128,1536]{1,0:T(8,128)(2,1)}, bf16[128,1536]{1,0:T(8,128)(2,1)}, bf16[2,48,1536]{2,1,0:T(8,128)(2,1)}, f32[8,3328]{1,0:T(8,128)}, f32[8,640]{1,0:T(8,128)}) custom-call(bf16[2,2,2,128,1536]{4,3,2,1,0:T(8,128)(2,1)} %bitcast.109, bf16[2,128,1536]{2,1,0:T(8,128)(2,1)} %tok.5, bf16[2,2,2,128,1536]{4,3,2,1,0:T(8,128)(2,1)} %get-tuple-element.60.eall, ...), custom_call_target="tpu_custom_call" | custom-call | tf_op jit(solution)/shard_map/last_sums/pallas_call | solution.py:710
  316.1 0.8 slice.151
  317.6 1.8 pad_maximum_fusion.1
  319.4 10.9 %all-to-all-start.1 = ((bf16[8,24,1536]{2,1,0:T(8,128)(2,1)}), bf16[8,24,1536]{2,1,0:T(8,128)(2,1)S(1)}, u32[]{:S(2)}, u32[]{:S(2)}) async-start(bf16[8,24,1536]{2,1,0:T(8,128)(2,1)} %bitcast.37), calls=%async_computation.1 | async-start | bytes 1179648 | tf_op jit(solution)/shard_map/all_to_all | solution.py:1209
  330.3 1.0 broadcast_select_fusion
  331.4 1.5 collective-permute-start.1
  332.9 0.9 slice.152
  333.8 0.8 constant_dynamic-slice_fusion.1
  338.1 9.3 %collective-permute-done.1 = bf16[128,1536]{1,0:T(8,128)(2,1)S(1)} collective-permute-done((bf16[128,1536]{1,0:T(8,128)(2,1)S(1)}, bf16[128,1536]{1,0:T(8,128)(2,1)S(1)}, u32[]{:S(2)}, u32[]{:S(2)}) %collective-permute-start.1) | collective-permute-done | bytes 393248 | tf_op jit(solution)/shard_map/ppermute | solution.py:1213
  347.5 3.0 fusion
  351.4 1.0 fusion.1
  (87 shorter events, 14.2 us)
Async XLA Ops:
  0.6 14.6 %copy-start.6 = (f32[1,48]{1,0:T(1,128)S(1)}, f32[1,48]{1,0:T(1,128)}, u32[]{:S(2)}) copy-start(f32[1,48]{1,0:T(1,128)} %param.19) | copy-start | bytes 580
  0.7 14.6 %copy-start.5 = (f32[1,48]{1,0:T(1,128)S(1)}, f32[1,48]{1,0:T(1,128)}, u32[]{:S(2)}) copy-start(f32[1,48]{1,0:T(1,128)} %param.20) | copy-start | bytes 580
  0.7 14.6 %copy-start.4 = (f32[1,48]{1,0:T(1,128)S(1)}, f32[1,48]{1,0:T(1,128)}, u32[]{:S(2)}) copy-start(f32[1,48]{1,0:T(1,128)} %param.21) | copy-start | bytes 580
  9.3 15.2 %all-to-all-start = ((bf16[8,24,1536]{2,1,0:T(8,128)(2,1)}), bf16[8,24,1536]{2,1,0:T(8,128)(2,1)S(1)}, u32[]{:S(2)}, u32[]{:S(2)}) async-start(bf16[8,24,1536]{2,1,0:T(8,128)(2,1)} %bitcast.6), calls=%async_computation | async-start | bytes 1179648 | tf_op jit(solution)/shard_map/all_to_all | solution.py:1166
  15.3 8.7 %collective-permute-start = (f32[3,48]{1,0:T(4,128)S(1)}, f32[3,48]{1,0:T(4,128)S(1)}, u32[]{:S(2)}, u32[]{:S(2)}) collective-permute-start(f32[3,48]{1,0:T(4,128)S(1)} %get-tuple-element.98), channel_id=1, source_target_pairs={{0,64},{64,0},{1,65},{65,1},{2,66},{66,2},{3,67},{67,3},{4,68},{68... | collective-permute-start | bytes 1736 | tf_op jit(solution)/shard_map/ppermute | solution.py:1177
  260.1 57.5 %copy-start.3 = (bf16[2,48,1536]{2,1,0:T(8,128)(2,1)S(1)}, bf16[2,48,1536]{2,1,0:T(8,128)(2,1)}, u32[]{:S(2)}) copy-start(bf16[2,48,1536]{2,1,0:T(8,128)(2,1)} %get-tuple-element.74) | copy-start | bytes 884740
  316.1 31.4 %copy-start = (bf16[128,1536]{1,0:T(8,128)(2,1)S(1)}, bf16[128,1536]{1,0:T(8,128)(2,1)}, u32[]{:S(2)}) copy-start(bf16[128,1536]{1,0:T(8,128)(2,1)} %get-tuple-element.72) | copy-start | bytes 1179652
  316.1 31.4 %copy-start.1 = (bf16[128,1536]{1,0:T(8,128)(2,1)S(1)}, bf16[128,1536]{1,0:T(8,128)(2,1)}, u32[]{:S(2)}) copy-start(bf16[128,1536]{1,0:T(8,128)(2,1)} %get-tuple-element.71) | copy-start | bytes 1179652
  319.4 31.0 %all-to-all-start.1 = ((bf16[8,24,1536]{2,1,0:T(8,128)(2,1)}), bf16[8,24,1536]{2,1,0:T(8,128)(2,1)S(1)}, u32[]{:S(2)}, u32[]{:S(2)}) async-start(bf16[8,24,1536]{2,1,0:T(8,128)(2,1)} %bitcast.37), calls=%async_computation.1 | async-start | bytes 1179648 | tf_op jit(solution)/shard_map/all_to_all | solution.py:1209
  331.4 16.1 %collective-permute-start.1 = (bf16[128,1536]{1,0:T(8,128)(2,1)S(1)}, bf16[128,1536]{1,0:T(8,128)(2,1)S(1)}, u32[]{:S(2)}, u32[]{:S(2)}) collective-permute-start(bf16[128,1536]{1,0:T(8,128)(2,1)S(1)} %broadcast_select_fusion), channel_id=1, source_target_pairs={{0,64},{64,0},{1,65},{65,1},{2,66},{66,2},{3,67},{67,3},{4,68},{68... | collective-permute-start | bytes 1179656 | tf_op jit(solution)/shard_map/ppermute | solution.py:1213
  350.4 1.0 copy-start.2
  350.4 2.0 copy-start.7
where the time goes:
time: 358 us; the launch traced here: 354 us
  Pallas kernels  283 us (79%)
  local copies, waits for them, and re-layouts  22.2 us (6%)
  starting transfers between devices  19.8 us (6%)
  waiting for transfers between devices  16.7 us (5%)
  other arithmetic  11.1 us (3%)
    pallas_call x1, Pallas kernels, backward_sum(): pl.pallas_call(kernel, name='backward_sum', out_shape=(CHUNKS, jax.ShapeD...  57.3 us
    pallas_call x1, Pallas kernels, last_sums(): pl.pallas_call(kernel, name='last_sums', out_shape=(CHUNK, CHUNK, jax.Sha...  56 us
    pallas_call x1, Pallas kernels, forward_sum(): pl.pallas_call(kernel, name='forward_sum', out_shape=(CHUNKS, GATHERED, j...  49.5 us
    pallas_call x2, Pallas kernels, layer_backward(): pl.pallas_call(make_backward(first), name='layer_backward', grid=(4,), in...  44.2 us
    pallas_call x1, Pallas kernels, first_gathers(): pl.pallas_call(kernel, name='first_gathers', out_shape=(GATHERED, CHUNKS,...  36.5 us
    pallas_call x2, Pallas kernels, layer_forward(): pl.pallas_call(make_forward(with_do), name='layer_forward', grid=(4,), in...  31.6 us
    all_to_all x1, starting transfers between devices, body(): lax.all_to_all(jnp.stack([gs0, gs1]).reshape(8, 24, D), GROUP, 0, 0, tile...  10.9 us
    ppermute x1, waiting for transfers between devices, body(): got = lax.ppermute(jnp.where(s == 0, so1, ig0), 's', [(0, 1), (1, 0)])  9.34 us
  transfers between devices with their start and end apart: 4, of which 3 were waited for; matrix products, arithmetic and copies ran while one was open for 3% of the time, Pallas kernels for 0%

commit v1 on v0

--- a/solution.py
+++ b/solution.py
@@ -28,7 +28,7 @@
     def __init__(self, ssem, rsem):
         self.ssem, self.rsem, self.n, self.all = ssem, rsem, 0, []
 
-    def send(self, src, dst, dev):
+    def make(self, src, dst, dev):
         i = self.n
         self.n += 1
         assert i < self.ssem.shape[0]
@@ -40,8 +40,12 @@
             device_id=dev,
             device_id_type=pl.DeviceIdType.MESH,
         )
+        self.all.append(copy)
+        return copy
+
+    def send(self, src, dst, dev):
+        copy = self.make(src, dst, dev)
         copy.start()
-        self.all.append(copy)
         return copy
 
     def finish(self):
@@ -227,7 +231,7 @@
     local.wait()
 
 
-NSUB = 4
+NSUB = 1
 SUBT = 9.25 / NSUB
 ROWS = 128 // NSUB
 PART = ROWS // 2
@@ -560,61 +564,6 @@
     return copy
 
 
-def forward_sum(part, stat, tok, blk):
-    def kernel(part, stat, tok, blk, xall, w, total, fin, xo, cb, sb, b1, b2, stb, lsem, ssem, rsem):
-        greet(zx_devs() + group_devs())
-        net = Net(ssem, rsem)
-        s, z, h, x, c = place()
-        own = Once(pltpu.make_async_copy(tok.at[s], xo, lsem.at[0]))
-
-        def done(rows, v):
-            own.wait()
-            scale = own_scale(total)[rows.start : rows.start + rows.size]
-            fin[rows] = (xo[rows].astype(F32) + scale * v).astype(BF)
-
-        def chain(sub):
-            yield from g_xrs(net, part, (cb, sb, b1, b2), done, sub)
-            yield from g_yag(net, fin, xall, lsem.at[2 + sub], sub)
-
-        run(
-            [g_stats(net, stat, total, stb)]
-            + [chain(sub) for sub in range(NSUB)]
-            + [g_ag(net, blk, w, lsem.at[1])]
-        )
-        net.finish()
-
-    return pl.pallas_call(
-        kernel,
-        name="forward_sum",
-        out_shape=(CHUNKS, GATHERED, jax.ShapeDtypeStruct((8, 128), F32)),
-        in_specs=[VM, VM, ANY, VM],
-        out_specs=(ANY, ANY, VM),
-        scratch_shapes=[pltpu.VMEM((128, D), BF), pltpu.VMEM((128, D), BF)]
-        + xrs_scratch()
-        + [pltpu.VMEM((7, 8, 128), F32), pltpu.SemaphoreType.DMA((2 + NSUB,))]
-        + sems(39 + 18 * NSUB),
-        compiler_params=params(1),
-    )(part, stat, tok, blk)
-
-
-def stats_sum(stat):
-    def kernel(stat, total, stb, ssem, rsem):
-        greet(group_devs())
-        net = Net(ssem, rsem)
-        run([g_stats(net, stat, total, stb)])
-        net.finish()
-
-    return pl.pallas_call(
-        kernel,
-        name="stats_sum",
-        out_shape=jax.ShapeDtypeStruct((16, 128), F32),
-        in_specs=[VM],
-        out_specs=VM,
-        scratch_shapes=[pltpu.VMEM((7, 16, 128), F32)] + sems(8),
-        compiler_params=params(2),
-    )(stat)
-
-
 def norm_back(v, x, e, ng):
     xf = x.astype(F32)
     vg = v * ng[...]
@@ -805,66 +754,6 @@
     return cv[...]
 
 
-def front(xb, w, ng, u_out):
-    xf = xb[...].astype(F32)
-    r = lax.rsqrt(jnp.mean(xf * xf, axis=-1, keepdims=True) + EPS)
-    u = (xf * r * ng[...]).astype(BF)
-    u_out[...] = u
-    return jnp.dot(u, w[:, 0:CIN], preferred_element_type=F32)
-
-
-def make_forward(with_do):
-    def kernel(st, x, w, ng, cv, *rest):
-        if with_do:
-            e, part, stat, proj, yout, uout, doo, og = rest
-        else:
-            part, stat, proj, yout, uout, og = rest
-        step = pl.program_id(0)
-        proj[...] = front(x, w, ng, uout)
-        if with_do:
-            doo[...] = jnp.dot(e[...], w[:, CIN:D], preferred_element_type=F32)
-        low = half_masks()
-        for m in range(2):
-            rows = slice(128 * m, 128 * m + 128)
-            chunk = step * 2 + m
-            keep, valid = masks(st, chunk)
-            act = []
-            for t in range(5):
-                pre, _ = conv_tile(proj[rows, HC + 128 * t : HC + 128 * t + 128], cv, t, valid)
-                act.append((pre * jax.nn.sigmoid(pre)).astype(BF))
-            _, dt, cum = rates(proj[rows, RT:CIN], cv)
-            cum_t, dt_t = jnp.transpose(cum), jnp.transpose(dt)
-            gram = nt(act[4], act[3])
-            gsum = jnp.zeros((128, 1), F32)
-            tsum = jnp.zeros((128, 1), F32)
-            for t in range(3):
-                lanes = slice(128 * t, 128 * t + 128)
-                mixes = []
-                for h in (2 * t, 2 * t + 1):
-                    dec = decay_of(keep, cum, cum_t, h)
-                    mixes.append((gram * dec * dt_t[h : h + 1, :]).astype(BF))
-                y = jnp.dot(
-                    jnp.concatenate(mixes, axis=1),
-                    split_pair(act[t], low),
-                    preferred_element_type=F32,
-                )
-                y = y + cv[6:7, lanes] * act[t].astype(F32)
-                yout[rows, lanes] = y
-                zt = proj[rows, lanes]
-                g = y * (zt * jax.nn.sigmoid(zt))
-                gsum = gsum + jnp.sum(g * g, axis=1, keepdims=True)
-                gain = cv[5:6, lanes]
-                og[rows, lanes] = (g * gain).astype(BF)
-                if with_do:
-                    tsum = tsum + jnp.sum(g * gain * doo[rows, lanes], axis=1, keepdims=True)
-            stat[pl.ds(chunk, 1), :] = col_to_row(gsum)
-            if with_do:
-                stat[pl.ds(chunk + 8, 1), :] = col_to_row(tsum)
-        part[...] = nt(og[...], w[:, CIN:D]).astype(BF)
-
-    return kernel
-
-
 def rows_spec(cols):
     return pl.BlockSpec((256, cols), lambda i: (i, 0))
 
@@ -873,37 +762,402 @@
     return pl.BlockSpec(shape, lambda i: (0,) * len(shape))
 
 
-def layer_forward(st, x, w, ng, cv, e=None):
+class Gather:
+    def __init__(self, net, blk, out, lsem):
+        s, z, h, x, c = place()
+        self.local = pltpu.make_async_copy(blk, out.at[z, :, x], lsem)
+        every = slice(None)
+        self.parts = []
+        for lanes, i, axis_i, j, axis_j, pick in (
+            (pl.ds(0, HALF), x, "x", z, "z", lambda i, j, p: (j, p, i)),
+            (pl.ds(HALF, HALF), z, "z", x, "x", lambda i, j, p: (i, p, j)),
+        ):
+            ir, il, _ = ring(i)
+            jr, jl, _ = ring(j)
+
+            def at(i, j, p, pick=pick, lanes=lanes):
+                return out.at[pick(i, j, p) + (every, lanes)]
+
+            def make(i, j, p, dev, src=None):
+                ref = at(i, j, p)
+                return net.make(ref if src is None else src, ref, dev)
+
+            own = blk.at[:, :, lanes]
+            first, second = ({axis_i: ir}, {axis_i: il}), ({axis_j: jr}, {axis_j: jl})
+            self.parts.append(
+                [
+                    (make(i, j, every, first[0], own), make(i, j, every, first[1], own)),
+                    (make(il, j, 0, first[0]), make(ir, j, 1, first[1])),
+                    (make(every, j, every, second[0]), make(every, j, every, second[1])),
+                    (make(every, jl, 0, second[0]), make(every, jr, 1, second[1])),
+                ]
+            )
+
+    def step(self, k):
+        if k == 0:
+            self.local.start()
+        if k == 2:
+            self.local.wait()
+        for part in self.parts:
+            for n in range(2):
+                if k > 0:
+                    part[k - 1][n].wait_recv()
+                if k < 4 and k != 2:
+                    part[k][n].start()
+            if k == 2:
+                part[2][0].start()
+                part[2][1].start()
+
+
+class RingSum:
+    def __init__(self, net, part, bufs):
+        self.part = part
+        self.cb, self.sb, self.b1, self.b2 = bufs
+        s, z, h, x, c = place()
+        self.c = c
+        sib = {"c": 1 - c}
+        outer, inner = {"h": 1 - h, "s": 1 - s}, {"s": 1 - s}
+        self.units = [(1 - h, s), (1 - h, 1 - s), (h, 1 - s), (h, s)]
+        self.core = [
+            net.make(part.at[hh, 1 - c, mm], self.cb.at[k], sib)
+            for k, (hh, mm) in enumerate(self.units)
+        ]
+        sb, b1, b2 = self.sb, self.b1, self.b2
+        lo, hi = pl.ds(0, 64), pl.ds(64, 64)
+        self.far = [
+            net.make(sb.at[0, lo], b1.at[0], outer),
+            net.make(sb.at[0, hi], b1.at[1], inner),
+        ]
+        self.direct = [
+            net.make(sb.at[1, lo], b2.at[0, lo], outer),
+            net.make(sb.at[2, hi], b2.at[1, hi], inner),
+        ]
+        self.summed = [
+            net.make(sb.at[1, hi], b2.at[0, hi], outer),
+            net.make(sb.at[2, lo], b2.at[1, lo], inner),
+        ]
+
+    def core_send(self, ks):
+        for k in ks:
+            self.core[k].start()
+
+    def add(self, k):
+        self.core[k].wait_recv()
+        hh, mm = self.units[k]
+        self.sb[k] = (self.part[hh, self.c, mm].astype(F32) + self.cb[k].astype(F32)).astype(BF)
+
+    def early(self):
+        self.add(0)
+        self.far[0].start()
+        self.far[1].start()
+        self.add(1)
+        self.direct[0].start()
+
+    def late(self):
+        self.add(2)
+        self.direct[1].start()
+        lo, hi = slice(0, 64), slice(64, 128)
+        self.far[1].wait_recv()
+        self.sb[1, hi] = (self.sb[1, hi].astype(F32) + self.b1[1].astype(F32)).astype(BF)
+        self.summed[0].start()
+        self.far[0].wait_recv()
+        self.sb[2, lo] = (self.sb[2, lo].astype(F32) + self.b1[0].astype(F32)).astype(BF)
+        self.summed[1].start()
+
+    def total(self):
+        self.core[3].wait_recv()
+        for copy in self.direct + self.summed:
+            copy.wait_recv()
+        hh, mm = self.units[3]
+        total = self.part[hh, self.c, mm].astype(F32) + self.cb[3].astype(F32)
+        return total + self.b2[0].astype(F32) + self.b2[1].astype(F32)
+
+
+def ring_scratch():
+    return [
+        pltpu.VMEM((4, 128, D), BF),
+        pltpu.VMEM((3, 128, D), BF),
+        pltpu.VMEM((2, 64, D), BF),
+        pltpu.VMEM((2, 128, D), BF),
+    ]
+
+
+class Spread:
+    def __init__(self, net, out):
+        s, z, h, x, c = place()
+        sib = {"c": 1 - c}
+        outer, inner = {"h": 1 - h, "s": 1 - s}, {"s": 1 - s}
+        lo, hi = pl.ds(0, 64), pl.ds(64, 64)
+        own, far = out.at[h, c, s], out.at[1 - h, c, s]
+        from_outer, from_inner = out.at[1 - h, c, 1 - s], out.at[h, c, 1 - s]
+        self.mine = own
+        self.ring = [net.make(own, own, outer), net.make(own, own, inner)]
+        self.hand = [
+            net.make(from_inner.at[lo], from_inner.at[lo], outer),
+            net.make(from_outer.at[hi], from_outer.at[hi], inner),
+        ]
+        self.sib = [net.make(r, r, sib) for r in (own, from_inner, from_outer, far)]
+
+    def start(self):
+        self.ring[0].start()
+        self.ring[1].start()
+        self.sib[0].start()
+
+    def hand_on(self):
+        self.ring[1].wait_recv()
+        self.hand[0].start()
+        self.ring[0].wait_recv()
+        self.hand[1].start()
+        self.sib[1].start()
+        self.sib[2].start()
+
+    def wait_same(self):
+        self.sib[0].wait_recv()
+        self.sib[1].wait_recv()
+
+    def wait_far(self):
+        self.hand[0].wait_recv()
+        self.hand[1].wait_recv()
+        self.sib[3].start()
+
+    def wait_other(self):
+        self.sib[2].wait_recv()
+        self.sib[3].wait_recv()
+
+
+def block_at(i, h, c, other_first):
+    first = 1 if other_first else 0
+    hi = lax.rem(h + first + i // 2, 2)
+    ci = lax.rem(c + (i + first if other_first else i), 2)
+    return hi, ci
+
+
+def forward_block(b, chunk_rows, x, w, ng, cv, st, refs, e=None):
+    part, stat, proj, yout, uout, doo, og = refs
     with_do = e is not None
-    n_stat = 16 if with_do else 8
-    ins = [st, x, w, ng, cv] + ([e] if with_do else [])
-    in_specs = [SM, rows_spec(D), whole(D, D), whole(1, D), whole(16, 640)] + (
-        [rows_spec(D)] if with_do else []
-    )
-    outs = [
-        jax.ShapeDtypeStruct((1024, D), BF),
-        jax.ShapeDtypeStruct((n_stat, 128), F32),
-        jax.ShapeDtypeStruct((1024, CIN), F32),
-        jax.ShapeDtypeStruct((1024, HC), F32),
-        jax.ShapeDtypeStruct((1024, D), BF),
-    ] + ([jax.ShapeDtypeStruct((1024, HC), F32)] if with_do else [])
-    out_specs = [
-        rows_spec(D),
-        whole(n_stat, 128),
-        rows_spec(CIN),
-        rows_spec(HC),
-        rows_spec(D),
-    ] + ([rows_spec(HC)] if with_do else [])
+    xf = x[...].reshape(256, D).astype(F32)
+    r = lax.rsqrt(jnp.mean(xf * xf, axis=-1, keepdims=True) + EPS)
+    u = (xf * r * ng).astype(BF)
+    uout[...] = u
+    proj[...] = jnp.dot(u, w[:, :, :, :, 0:CIN].reshape(D, CIN), preferred_element_type=F32)
+    if with_do:
+        doo[...] = jnp.dot(
+            e[...].reshape(256, D),
+            w[:, :, :, :, CIN:D].reshape(D, HC),
+            preferred_element_type=F32,
+        )
+    low = half_masks()
+    for m in range(2):
+        rows = slice(128 * m, 128 * m + 128)
+        chunk = b * 2 + m
+        keep, valid = masks(st, chunk)
+        act = []
+        for t in range(5):
+            pre, _ = conv_tile(proj[rows, HC + 128 * t : HC + 128 * t + 128], cv, t, valid)
+            act.append((pre * jax.nn.sigmoid(pre)).astype(BF))
+        _, dt, cum = rates(proj[rows, RT:CIN], cv)
+        cum_t, dt_t = jnp.transpose(cum), jnp.transpose(dt)
+        gram = nt(act[4], act[3])
+        gsum = jnp.zeros((128, 1), F32)
+        tsum = jnp.zeros((128, 1), F32)
+        for t in range(3):
+            lanes = slice(128 * t, 128 * t + 128)
+            mixes = []
+            for h in (2 * t, 2 * t + 1):
+                dec = decay_of(keep, cum, cum_t, h)
+                mixes.append((gram * dec * dt_t[h : h + 1, :]).astype(BF))
+            y = jnp.dot(
+                jnp.concatenate(mixes, axis=1),
+                split_pair(act[t], low),
+                preferred_element_type=F32,
+            )
+            y = y + cv[6:7, lanes] * act[t].astype(F32)
+            yout[rows, lanes] = y
+            zt = proj[rows, lanes]
+            g = y * (zt * jax.nn.sigmoid(zt))
+            gsum = gsum + jnp.sum(g * g, axis=1, keepdims=True)
+            gain = cv[5:6, lanes]
+            og[rows, lanes] = (g * gain).astype(BF)
+            if with_do:
+                tsum = tsum + jnp.sum(g * gain * doo[rows, lanes], axis=1, keepdims=True)
+        stat[pl.ds(chunk, 1), :] = col_to_row(gsum)
+        if with_do:
+            stat[pl.ds(chunk + 8, 1), :] = col_to_row(tsum)
+    out = nt(og[...], w[:, :, :, :, CIN:D].reshape(D, HC))
+    part[...] = out.astype(BF).reshape(2, 128, D)
+
+
+def two_forward(st, x0, w0, ng, cv, call, blk):
+    def kernel(
+        st, x0h, w0h, ng, cv, callh, blk,
+        w1o, x1o, s0o, s1o, p1o, proj0o, proj1o, y0o, y1o, u0o, u1o, doo,
+        w0, w1, x0, x1, e1, part, part1, proj, yv, uv, dov, og, stat0, stat1, stb0, stb1,
+        cb, sb, b1, b2, isem, osem, lsem, ssem, rsem,
+    ):
+        s, z, h, x, c = place()
+        loads = [pltpu.make_async_copy(w0h, w0, isem.at[0]), pltpu.make_async_copy(callh, e1, isem.at[1])]
+        loads[0].start()
+        xl = [pltpu.make_async_copy(x0h.at[k // 2, k % 2], x0.at[k // 2, k % 2], isem.at[2 + k]) for k in range(4)]
+        for copy in xl:
+            copy.start()
+        greet(zx_devs() + group_devs())
+        net = Net(ssem, rsem)
+        gather = Gather(net, blk, w1, lsem.at[0])
+        ring = RingSum(net, part, (cb, sb, b1, b2))
+        spread = Spread(net, x1)
+        devs = group_devs()
+        stats0 = [net.make(stat0, stb0.at[k], dev) for k, dev in enumerate(devs)]
+        stats1 = [net.make(stat1, stb1.at[k], dev) for k, dev in enumerate(devs)]
+        gather.step(0)
+        loads[0].wait()
+        loads[1].start()
+        for copy in xl:
+            copy.wait()
+
+        def saves(b, layer, proj_o, y_o, u_o):
+            return [
+                pltpu.make_async_copy(v.at[b], o.at[b], osem.at[layer, n, b])
+                for n, (v, o) in enumerate(((proj, proj_o), (yv, y_o), (uv, u_o)))
+            ]
+
+        def first(i, carry):
+            hi, ci = block_at(i, h, c, True)
+            b = 2 * hi + ci
+            forward_block(
+                b, None, x0.at[hi, ci], w0, ng[0], cv.at[0], st,
+                (part.at[hi, ci], stat0, proj.at[b], yv.at[b], uv.at[b], None, og),
+            )
+            for copy in saves(b, 0, proj0o, y0o, u0o):
+                copy.start()
+
+            @pl.when(i == 0)
+            def _():
+                ring.core_send((0, 1))
+
+            @pl.when(i == 1)
+            def _():
+                ring.early()
+                gather.step(1)
+
+            @pl.when(i == 2)
+            def _():
+                ring.core_send((2, 3))
+                gather.step(2)
+
+            return carry
+
+        lax.fori_loop(0, 4, first, 0)
+        for copy in stats0:
+            copy.start()
+        ring.late()
+        acc = stat0[...]
+        for k, copy in enumerate(stats0):
+            copy.wait_recv()
+            acc = acc + stb0[k]
+        s0o[...] = acc
+        for b in range(4):
+            for copy in saves(b, 0, proj0o, y0o, u0o):
+                copy.wait()
+        loads[1].wait()
+        gather.step(3)
+        total = ring.total()
+        x1[h, c, s] = (x0[h, c, s].astype(F32) + own_scale(s0o) * total).astype(BF)
+        spread.start()
+        gather.step(4)
+        keep_w = pltpu.make_async_copy(w1, w1o, isem.at[0])
+        keep_w.start()
+        spread.hand_on()
+
+        def second(i, carry):
+            @pl.when(i == 1)
+            def _():
+                spread.wait_same()
+
+            @pl.when(i == 2)
+            def _():
+                spread.wait_far()
+
+            @pl.when(i == 3)
+            def _():
+                spread.wait_other()
+
+            hi, ci = block_at(i, h, c, False)
+            b = 2 * hi + ci
+            forward_block(
+                b, None, x1.at[hi, ci], w1, ng[1], cv.at[1], st,
+                (part1.at[hi, ci], stat1, proj.at[b], yv.at[b], uv.at[b], dov.at[b], og),
+                e1.at[hi, ci],
+            )
+            for copy in saves(b, 1, proj1o, y1o, u1o):
+                copy.start()
+            for n, (v, o) in enumerate(((dov.at[b], doo.at[b]), (x1.at[hi, ci], x1o.at[hi, ci]), (part1.at[hi, ci], p1o.at[hi, ci]))):
+                pltpu.make_async_copy(v, o, osem.at[2, n, b]).start()
+            return carry
+
+        lax.fori_loop(0, 4, second, 0)
+        for copy in stats1:
+            copy.start()
+        acc = stat1[...]
+        for k, copy in enumerate(stats1):
+            copy.wait_recv()
+            acc = acc + stb1[k]
+        s1o[...] = acc
+        keep_w.wait()
+        for b in range(4):
+            for copy in saves(b, 1, proj1o, y1o, u1o):
+                copy.wait()
+            p = (b // 2, b % 2)
+            for n, (v, o) in enumerate(((dov.at[b], doo.at[b]), (x1.at[p], x1o.at[p]), (part1.at[p], p1o.at[p]))):
+                pltpu.make_async_copy(v, o, osem.at[2, n, b]).wait()
+        net.finish()
+
+    blocks = lambda cols, t: jax.ShapeDtypeStruct((4, 256, cols), t)
     return pl.pallas_call(
-        make_forward(with_do),
-        name="layer_forward",
-        grid=(4,),
-        in_specs=in_specs,
-        out_specs=out_specs,
-        out_shape=outs,
-        scratch_shapes=[pltpu.VMEM((256, HC), BF)],
-        compiler_params=pltpu.CompilerParams(vmem_limit_bytes=VLIM),
-    )(*ins)
+        kernel,
+        name="two_forward",
+        out_shape=(
+            GATHERED,
+            CHUNKS,
+            jax.ShapeDtypeStruct((8, 128), F32),
+            jax.ShapeDtypeStruct((16, 128), F32),
+            CHUNKS,
+            blocks(CIN, F32),
+            blocks(CIN, F32),
+            blocks(HC, F32),
+            blocks(HC, F32),
+            blocks(D, BF),
+            blocks(D, BF),
+            blocks(HC, F32),
+        ),
+        in_specs=[SM, ANY, ANY, VM, VM, ANY, VM],
+        out_specs=(ANY, ANY, VM, VM) + (ANY,) * 8,
+        scratch_shapes=[
+            pltpu.VMEM((4, 2, 4, 48, D), BF),
+            pltpu.VMEM((4, 2, 4, 48, D), BF),
+            pltpu.VMEM((2, 2, 2, 128, D), BF),
+            pltpu.VMEM((2, 2, 2, 128, D), BF),
+            pltpu.VMEM((2, 2, 2, 128, D), BF),
+            pltpu.VMEM((2, 2, 2, 128, D), BF),
+            pltpu.VMEM((2, 2, 2, 128, D), BF),
+            pltpu.VMEM((4, 256, CIN), F32),
+            pltpu.VMEM((4, 256, HC), F32),
+            pltpu.VMEM((4, 256, D), BF),
+            pltpu.VMEM((4, 256, HC), F32),
+            pltpu.VMEM((256, HC), BF),
+            pltpu.VMEM((8, 128), F32),
+            pltpu.VMEM((16, 128), F32),
+            pltpu.VMEM((7, 8, 128), F32),
+            pltpu.VMEM((7, 16, 128), F32),
+        ]
+        + ring_scratch()
+        + [
+            pltpu.SemaphoreType.DMA((6,)),
+            pltpu.SemaphoreType.DMA((3, 3, 4)),
+            pltpu.SemaphoreType.DMA((1,)),
+        ]
+        + sems(56),
+        compiler_params=params(1),
+    )(st, x0, w0, ng, cv, call, blk)
 
 
 def make_backward(first):
@@ -1177,17 +1431,18 @@
     other = lax.ppermute(heads, "s", [(0, 1), (1, 0)])
     heads = jnp.where(s == 0, jnp.stack([heads, other]), jnp.stack([other, heads]))
 
-    w0, tall, call = first_gathers(blk0, tokens, cotangent)
-    w0 = w0.reshape(D, D)
+    w0g, tall, call = first_gathers(blk0, tokens, cotangent)
+    w0 = w0g.reshape(D, D)
     x0 = tall.reshape(1024, D)
     e1 = call.reshape(1024, D)
     cv, ng = constants(w0, q, heads[:, 0], heads[:, 1], heads[:, 2])
-    part, stat0, proj0, y0, u0 = layer_forward(st, x0, w0, ng[0], cv[0])
-    xall, w1, stat0 = forward_sum(part.reshape(2, 2, 2, 128, D), stat0, tokens, blocks[1])
+    w1, xall, stat0, stat1, part1, proj0, proj1, y0, y1, u0, u1, do1 = two_forward(
+        st, tall, w0g, ng, cv, call, blocks[1]
+    )
+    flat = lambda v: v.reshape(1024, v.shape[-1])
+    proj0, proj1, y0, y1, u0, u1, do1 = map(flat, (proj0, proj1, y0, y1, u0, u1, do1))
     w1 = w1.reshape(D, D)
     x1 = xall.reshape(1024, D)
-    part1, stat1, proj1, y1, u1, do1 = layer_forward(st, x1, w1, ng[1], cv[1], e1)
-    stat1 = stats_sum(stat1)
     dproj1, o1, dpart1, sm1 = layer_backward(st, e1, w1, cv[1], proj1, y1, stat1, do=do1)
     eall, gs1, sm1 = backward_sum(
         dpart1.reshape(2, 2, 2, 128, D), xall, cotangent, ng[1], (u1, e1, dproj1, o1), sm1
@@ -1199,7 +1454,7 @@
         tokens,
         eall,
         ng[0],
-        part1.reshape(2, 2, 2, 128, D),
+        part1,
         xall,
         stat1[0:8],
         (u0, e0, dproj0, o0),

time: 358 us -> 322 us (0.90)
  Pallas kernels: 283 us -> 255 us
  starting transfers between devices: 19.8 us -> 14.9 us
    pallas_call x4 -> x1, Pallas kernels: 88.8 us -> 59.1 us  [two_forward(): pl.pallas_call(kernel, name='two_forward', out_shape=(GATHERED, CHUNKS, j...]
    pallas_call x2, Pallas kernels: 44.2 us -> 54.3 us  [layer_backward(): pl.pallas_call(make_backward(first), name='layer_backward', grid=(4,), in...]
    ppermute x1, waiting for transfers between devices: 9.34 us -> 0.01 us  [body(): got = lax.ppermute(jnp.where(s == 0, so1, ig0), 's', [(0, 1), (1, 0)])]
    all_to_all x1, waiting for transfers between devices: 0.18 us -> 8.91 us  [body(): rec = lax.all_to_all(mine, GROUP, 0, 0, tiled=True)]
    ppermute x1, waiting for transfers between devices: 7.22 us -> 0.01 us  [body(): other = lax.ppermute(heads, 's', [(0, 1), (1, 0)])]
    pallas_call x1, Pallas kernels: 57.3 us -> 52.6 us  [backward_sum(): pl.pallas_call(kernel, name='backward_sum', out_shape=(CHUNKS, jax.ShapeD...]
    all_to_all x1, waiting for transfers between devices: 0.01 us -> 4.41 us  [body(): lax.all_to_all(jnp.stack([gs0, gs1]).reshape(8, 24, D), GROUP, 0, 0, tile...]
    pallas_call x1, Pallas kernels: 56 us -> 51.9 us  [last_sums(): pl.pallas_call(kernel, name='last_sums', out_shape=(CHUNK, CHUNK, jax.Sha...]
  transfers between devices with their start and end apart: 4 -> 4, of which waited for: 3 -> 2; matrix products, arithmetic and copies ran while one was open for 3% -> 6% of each run, Pallas kernels for 0% -> 0%
where the time goes in v1:
time: 322 us; the launch traced here: 318 us
  Pallas kernels  255 us (79%)
  local copies, waits for them, and re-layouts  22.3 us (7%)
  starting transfers between devices  14.9 us (5%)
  waiting for transfers between devices  13.3 us (4%)
  other arithmetic  11.8 us (4%)
    pallas_call x1, Pallas kernels, two_forward(): pl.pallas_call(kernel, name='two_forward', out_shape=(GATHERED, CHUNKS, j...  59.1 us
    pallas_call x2, Pallas kernels, layer_backward(): pl.pallas_call(make_backward(first), name='layer_backward', grid=(4,), in...  54.3 us
    pallas_call x1, Pallas kernels, backward_sum(): pl.pallas_call(kernel, name='backward_sum', out_shape=(CHUNKS, jax.ShapeD...  52.6 us
    pallas_call x1, Pallas kernels, last_sums(): pl.pallas_call(kernel, name='last_sums', out_shape=(CHUNK, CHUNK, jax.Sha...  51.9 us
    pallas_call x1, Pallas kernels, first_gathers(): pl.pallas_call(kernel, name='first_gathers', out_shape=(GATHERED, CHUNKS,...  37 us
    all_to_all x1, waiting for transfers between devices, body(): rec = lax.all_to_all(mine, GROUP, 0, 0, tiled=True)  8.91 us
    all_to_all x1, starting transfers between devices, body(): lax.all_to_all(jnp.stack([gs0, gs1]).reshape(8, 24, D), GROUP, 0, 0, tile...  7.53 us
  transfers between devices with their start and end apart: 4, of which 2 were waited for; matrix products, arithmetic and copies ran while one was open for 6% of the time, Pallas kernels for 0%

profile of v1, /device:TPU:1, one launch (start us, length us, event | category | flops | bytes accessed | tf_op | source)
XLA Modules:
  0.0 318.4 jit_solution(10725631320452245545)
XLA Ops:
  1.3 2.2 collective-permute-start
  4.2 0.7 slice.155
  4.9 1.0 fusion.7
  5.9 0.7 convert_reduce_fusion
  6.7 0.8 reshape_squeeze.4
  7.5 1.4 concatenate.35
  9.0 0.8 copy.87
  10.1 0.9 copy_bitcast_fusion
  11.1 1.0 concatenate.37
  12.2 5.1 %all-to-all-start = ((bf16[8,24,1536]{2,1,0:T(8,128)(2,1)}), bf16[8,24,1536]{2,1,0:T(8,128)(2,1)S(1)}, u32[]{:S(2)}, u32[]{:S(2)}) async-start(bf16[8,24,1536]{2,1,0:T(8,128)(2,1)} %bitcast.6), calls=%async_computation | async-start | bytes 1179648 | tf_op jit(solution)/shard_map/all_to_all | solution.py:1420
  17.6 8.9 %all-to-all-done = bf16[8,24,1536]{2,1,0:T(8,128)(2,1)S(1)} async-done(((bf16[8,24,1536]{2,1,0:T(8,128)(2,1)}), bf16[8,24,1536]{2,1,0:T(8,128)(2,1)S(1)}, u32[]{:S(2)}, u32[]{:S(2)}) %all-to-all-start) | async-done | bytes 589856 | tf_op jit(solution)/shard_map/all_to_all | solution.py:1420
  26.6 0.8 fusion.6
  27.4 0.8 bitcast_add_fusion.blk
  28.2 37.0 %first_gathers.1 = (bf16[4,2,4,48,1536]{4,3,2,1,0:T(8,128)(2,1)}, bf16[2,2,2,128,1536]{4,3,2,1,0:T(8,128)(2,1)}, bf16[2,2,2,128,1536]{4,3,2,1,0:T(8,128)(2,1)}) custom-call(bf16[2,48,1536]{2,1,0:T(8,128)(2,1)} %bitcast_add_fusion.blk, bf16[2,128,1536]{2,1,0:T(8,128)(2,1)} %tok.3, bf16[2,128,1536]{2,1,0:T(8,128)(2,1)} %cot.3), custom_call_target="tpu_custom_call" | custom-call | tf_op jit(solution)/shard_map/first_gathers/pallas_call | solution.py:532
  65.2 1.2 slice_convert_fusion
  71.5 59.1 %two_forward.1 = (bf16[4,2,4,48,1536]{4,3,2,1,0:T(8,128)(2,1)}, bf16[2,2,2,128,1536]{4,3,2,1,0:T(8,128)(2,1)}, f32[8,128]{1,0:T(8,128)}, f32[16,128]{1,0:T(8,128...) custom-call(s32[8,4]{1,0:T(8,128)} %reshape.261.st, ...), custom_call_target="tpu_custom_call" | custom-call | tf_op jit(solution)/shard_map/two_forward/pallas_call | solution.py:1115
  130.6 1.3 slice.140.st
  131.9 20.6 %layer_backward.2 = (bf16[1024,1152]{1,0:T(8,128)(2,1)}, bf16[1024,384]{1,0:T(8,128)(2,1)}, bf16[1024,1536]{1,0:T(8,128)(2,1)}, f32[8,640]{1,0:T(8,128)}) custom-call(s32[8,4]{1,0:T(8,128)} %reshape.261.st, bf16[1024,1536]{1,0:T(8,128)(2,1)} %bitcast.104, bf16[1536,1536]{1,0:T(8,128)(2,1)} %bitcast.109, f32[16,640]{1,0:T(8,128)} %get-tuple-element.87.cv, ...), custom_call_target="tpu_custom_call" | custom-call | tf_op jit(solution)/shard_map/layer_backward/pallas_call | solution.py:1297
  152.5 52.6 %backward_sum.1 = (bf16[2,2,2,128,1536]{4,3,2,1,0:T(8,128)(2,1)}, bf16[2,48,1536]{2,1,0:T(8,128)(2,1)}, f32[8,640]{1,0:T(8,128)}) custom-call(bf16[2,2,2,128,1536]{4,3,2,1,0:T(8,128)(2,1)} %bitcast.115, bf16[2,2,2,128,1536]{4,3,2,1,0:T(8,128)(2,1)} %get-tuple-element.45.xall, bf16[2,128,1536]{2,1,0:T(8,128)(2,1)} %cot.3, f32[1,1536]{1,0:T(1,128)} %get-tuple-element.85.ng, ...), custom_call_target="tpu_custom_call" | custom-call | tf_op jit(solution)/shard_map/backward_sum/pallas_call | solution.py:604
  205.1 33.7 %layer_backward.3 = (bf16[1024,1152]{1,0:T(8,128)(2,1)}, bf16[1024,384]{1,0:T(8,128)(2,1)}, bf16[1024,1536]{1,0:T(8,128)(2,1)}, f32[8,640]{1,0:T(8,128)}) custom-call(s32[8,4]{1,0:T(8,128)} %reshape.261.st, bf16[1024,1536]{1,0:T(8,128)(2,1)} %bitcast.102, bf16[1536,1536]{1,0:T(8,128)(2,1)} %bitcast.107, f32[16,640]{1,0:T(8,128)} %get-tuple-element.86.cv, ...), custom_call_target="tpu_custom_call" | custom-call | tf_op jit(solution)/shard_map/layer_backward/pallas_call | solution.py:1297
  238.8 51.9 %last_sums.1 = (bf16[128,1536]{1,0:T(8,128)(2,1)}, bf16[128,1536]{1,0:T(8,128)(2,1)}, bf16[2,48,1536]{2,1,0:T(8,128)(2,1)}, f32[8,3328]{1,0:T(8,128)}, f32[8,640]{1,0:T(8,128)}) custom-call(bf16[2,2,2,128,1536]{4,3,2,1,0:T(8,128)(2,1)} %bitcast.114, bf16[2,128,1536]{2,1,0:T(8,128)(2,1)} %tok.3, bf16[2,2,2,128,1536]{4,3,2,1,0:T(8,128)(2,1)} %get-tuple-element.56.eall, ...), custom_call_target="tpu_custom_call" | custom-call | tf_op jit(solution)/shard_map/last_sums/pallas_call | solution.py:659
  290.7 0.8 fusion.8
  291.5 0.7 slice.150
  292.2 0.9 slice.151
  293.1 1.1 broadcast_select_fusion
  294.3 1.8 pad_maximum_fusion.1
  296.1 0.8 constant_dynamic-slice_fusion.1
  298.6 7.5 %all-to-all-start.1 = ((bf16[8,24,1536]{2,1,0:T(8,128)(2,1)}), bf16[8,24,1536]{2,1,0:T(8,128)(2,1)S(1)}, u32[]{:S(2)}, u32[]{:S(2)}) async-start(bf16[8,24,1536]{2,1,0:T(8,128)(2,1)} %bitcast.43), calls=%async_computation.1 | async-start | bytes 1179648 | tf_op jit(solution)/shard_map/all_to_all | solution.py:1464
  308.0 3.0 fusion
  311.0 4.4 %all-to-all-done.1 = bf16[8,24,1536]{2,1,0:T(8,128)(2,1)S(1)} async-done(((bf16[8,24,1536]{2,1,0:T(8,128)(2,1)}), bf16[8,24,1536]{2,1,0:T(8,128)(2,1)S(1)}, u32[]{:S(2)}, u32[]{:S(2)}) %all-to-all-start.1) | async-done | bytes 589856 | tf_op jit(solution)/shard_map/all_to_all | solution.py:1464
  315.8 0.7 copy.111
  316.6 1.0 fusion.1
  (81 shorter events, 12.1 us)
Async XLA Ops:
  1.3 15.9 %collective-permute-start = (f32[3,48]{1,0:T(4,128)S(1)}, f32[3,48]{1,0:T(4,128)S(1)}, u32[]{:S(2)}, u32[]{:S(2)}) collective-permute-start(f32[3,48]{1,0:T(4,128)S(1)} %get-tuple-element.94), channel_id=1, source_target_pairs={{0,64},{64,0},{1,65},{65,1},{2,66},{66,2},{3,67},{67,3},{4,68},{68... | collective-permute-start | bytes 1736 | tf_op jit(solution)/shard_map/ppermute | solution.py:1431
  12.2 14.4 %all-to-all-start = ((bf16[8,24,1536]{2,1,0:T(8,128)(2,1)}), bf16[8,24,1536]{2,1,0:T(8,128)(2,1)S(1)}, u32[]{:S(2)}, u32[]{:S(2)}) async-start(bf16[8,24,1536]{2,1,0:T(8,128)(2,1)} %bitcast.6), calls=%async_computation | async-start | bytes 1179648 | tf_op jit(solution)/shard_map/all_to_all | solution.py:1420
  70.9 0.7 copy-start.3
  238.8 55.5 %copy-start.4 = (bf16[2,48,1536]{2,1,0:T(8,128)(2,1)S(1)}, bf16[2,48,1536]{2,1,0:T(8,128)(2,1)}, u32[]{:S(2)}) copy-start(bf16[2,48,1536]{2,1,0:T(8,128)(2,1)} %get-tuple-element.70) | copy-start | bytes 884740
  290.7 17.3 %copy-start = (bf16[128,1536]{1,0:T(8,128)(2,1)S(1)}, bf16[128,1536]{1,0:T(8,128)(2,1)}, u32[]{:S(2)}) copy-start(bf16[128,1536]{1,0:T(8,128)(2,1)} %get-tuple-element.68) | copy-start | bytes 1179652
  290.7 17.2 %copy-start.1 = (bf16[128,1536]{1,0:T(8,128)(2,1)S(1)}, bf16[128,1536]{1,0:T(8,128)(2,1)}, u32[]{:S(2)}) copy-start(bf16[128,1536]{1,0:T(8,128)(2,1)} %get-tuple-element.67) | copy-start | bytes 1179652
  294.2 13.8 %collective-permute-start.1 = (bf16[128,1536]{1,0:T(8,128)(2,1)S(1)}, bf16[128,1536]{1,0:T(8,128)(2,1)S(1)}, u32[]{:S(2)}, u32[]{:S(2)}) collective-permute-start(bf16[128,1536]{1,0:T(8,128)(2,1)S(1)} %broadcast_select_fusion), channel_id=1, source_target_pairs={{0,64},{64,0},{1,65},{65,1},{2,66},{66,2},{3,67},{67,3},{4,68},{68... | collective-permute-start | bytes 1179656 | tf_op jit(solution)/shard_map/ppermute | solution.py:1468
  298.6 16.8 %all-to-all-start.1 = ((bf16[8,24,1536]{2,1,0:T(8,128)(2,1)}), bf16[8,24,1536]{2,1,0:T(8,128)(2,1)S(1)}, u32[]{:S(2)}, u32[]{:S(2)}) async-start(bf16[8,24,1536]{2,1,0:T(8,128)(2,1)} %bitcast.43), calls=%async_computation.1 | async-start | bytes 1179648 | tf_op jit(solution)/shard_map/all_to_all | solution.py:1464
  311.0 5.7 %copy-start.2 = (bf16[1,24,6448]{2,1,0:T(8,128)(2,1)S(1)}, bf16[1,24,6448]{2,1,0:T(8,128)(2,1)}, u32[]{:S(2)}) copy-start(bf16[1,24,6448]{2,1,0:T(8,128)(2,1)} %param.16) | copy-start | bytes 928516
  315.5 2.1 copy-start.5
